TPU v7x, 512 devices: a whole 4x4x16 slice. The times are simulated.
512 devices in a mesh: row: 16 (over z), col: 32 (over y, x, core).
Axes of the slice: x: 4, y: 4, z: 16, core: 2. Of those that a mesh axis runs over, the one named last changes fastest.
Arguments:
- centroids: float32 [3, 32768], P(None, ('col', 'row')), may hold values from 0 to 1, as said below
- areas: float32 [32768], P(('col', 'row')), may hold values from 0.5 to 2
- conductance: float32 [32768], P(('col', 'row')), may hold values from 0.1 to 1
- power: float32 [16, 32768], P(None, ('col', 'row')), may hold values from -3 to 6
Outputs:
- solution: float32 [16, 32768], P(None, ('col', 'row'))
- residual: float32 [16, 32768], P(None, ('col', 'row'))
Inputs may be any that keep to these rules, and one draw needn't show every extreme that they name: `centroids`: panels lie on 16 parallel fins across the unit cube.
All inputs are finite; a program needn't handle non-finite values.
Results may differ from a plain program's by a relative error of at most 0.00039.
Values may be sent and summed in bfloat16 or wider, within the bound.
No kernel may reach another device: no remote copies, remote signals or barrier semaphores. Data moves between devices by JAX's collectives and lax.ppermute only.
A program may use at most 64 MiB of HBM per device.

v0:
```python
import math

import jax
import jax.numpy as jnp
from jax import lax
from jax.sharding import PartitionSpec as P


def kernel_tile(src, tgt, scale, delta2):
    dx = src[0][:, None] - tgt[0][None, :]
    dy = src[1][:, None] - tgt[1][None, :]
    dz = src[2][:, None] - tgt[2][None, :]
    dist2 = dx * dx + dy * dy + dz * dz
    return (src[3][:, None] * scale * lax.rsqrt(dist2 + delta2)).astype(jnp.bfloat16)


def inner(left, right):
    return jnp.dot(left, right.T, precision=lax.Precision.HIGHEST)


def lower_inverse(gram):
    factor = jnp.linalg.cholesky(gram)
    eye = jnp.eye(gram.shape[0], dtype=jnp.float32)
    return (factor, jax.scipy.linalg.solve_triangular(factor, eye, lower=True))


def reduce_small(terms):
    return lax.psum(terms, ("row", "col"))


def body(centroids, areas, conductance, power):
    high = lax.Precision.HIGHEST
    width = power.shape[1]
    nrhs = power.shape[0]
    panels = width * lax.axis_size("row") * lax.axis_size("col")
    scale = 4.0 / (math.pi * panels)
    delta2 = 16.0 / panels
    geom = jnp.concatenate([centroids, areas[None, :]], 0)
    sources = lax.all_gather(geom, "col", axis=1, tiled=True)
    targets = lax.all_gather(centroids, "row", axis=1, tiled=True)
    tgt_len = targets.shape[1]
    rhs, cond_row = (power, conductance[None, :])
    factor0, inverse0 = lower_inverse(reduce_small(inner(rhs, rhs)))
    basis = [jnp.dot(inverse0, rhs, precision=high)]
    blocks = {}
    for step in range(2):
        field = basis[step]
        empty = jnp.zeros((nrhs, tgt_len), jnp.float32)
        piece = lax.all_gather(field.astype(jnp.bfloat16), "col", axis=1, tiled=True)
        cols = piece.shape[1]
        step_len = width * max(1, 512 // width)
        turns = cols // step_len

        def one(turn, acc):
            vec = lax.dynamic_slice_in_dim(piece, turn * step_len, step_len, 1)
            src = lax.dynamic_slice_in_dim(sources, turn * step_len, step_len, 1)
            tile = kernel_tile(src, targets, scale, delta2)
            return acc + jnp.dot(vec, tile, preferred_element_type=jnp.float32)

        apply_total = lax.fori_loop(0, turns, one, empty)
        product = lax.psum_scatter(apply_total, "row", scatter_dimension=1, tiled=True)
        image = cond_row * field + product
        coeffs = list(reduce_small(tuple((inner(vec, image) for vec in basis))))
        for idx in range(step + 1):
            image = image - jnp.dot(coeffs[idx].T, basis[idx], precision=high)
        gram = reduce_small(inner(image, image))
        for idx in range(step + 1):
            blocks[idx, step] = coeffs[idx]
        factor, inverse = lower_inverse(gram)
        blocks[step + 1, step] = factor.T
        basis.append(jnp.dot(inverse, image, precision=high))
    hbar = jnp.zeros((3 * nrhs, 2 * nrhs), jnp.float32)
    for key in blocks:
        hbar = hbar.at[
            key[0] * nrhs : (key[0] + 1) * nrhs, key[1] * nrhs : (key[1] + 1) * nrhs
        ].set(blocks[key])
    target = jnp.zeros((3 * nrhs, nrhs), jnp.float32).at[:nrhs].set(factor0.T)
    normal = jnp.dot(hbar.T, hbar, precision=high)
    chol = jnp.linalg.cholesky(normal)
    coeff_y = jax.scipy.linalg.cho_solve((chol, True), jnp.dot(hbar.T, target, precision=high))
    coeff_z = target - jnp.dot(hbar, coeff_y, precision=high)
    solution = jnp.dot(coeff_y[:nrhs].T, basis[0], precision=high) + jnp.dot(
        coeff_y[nrhs:].T, basis[1], precision=high
    )
    residual = jnp.dot(coeff_z[:nrhs].T, basis[0], precision=high) + jnp.dot(
        coeff_z[nrhs : 2 * nrhs].T, basis[1], precision=high
    )
    residual = residual + jnp.dot(coeff_z[2 * nrhs :].T, basis[2], precision=high)
    return (solution, residual)


def solution(mesh):
    return jax.shard_map(
        body,
        mesh=mesh,
        in_specs=(
            P(None, ("col", "row")),
            P(("col", "row")),
            P(("col", "row")),
            P(None, ("col", "row")),
        ),
        out_specs=(P(None, ("col", "row")), P(None, ("col", "row"))),
        check_vma=False,
    )
```

profile of v0, /device:TPU:1, one launch (start us, length us, event | category | flops | bytes accessed | tf_op | source)
XLA Modules:
  0.0 797.1 jit_solution(8880030113008817273)
XLA Ops:
  8.0 111.0 %psum.42 = f32[16,16]{0,1:T(8,128)S(1)} all-reduce(f32[16,16]{0,1:T(8,128)S(1)} %fusion.59), channel_id=1, replica_groups=mesh['row'=16,'col'=32] {'row','col'}, use_global_device_ids=true, to_apply=%region_0.0 | all-reduce | flops 256 | bytes 2048 | tf_op jit(solution)/shard_map/psum | solution.py:28
  119.1 1.5 cholesky.94
  121.9 1.2 custom-call.20
  123.5 22.9 %all-gather = bf16[32,64,16]{1,2,0:T(8,128)(2,1)S(1)} all-gather(bf16[1,64,16]{1,2,0:T(8,128)(2,1)S(1)} %convert_bitcast_fusion.1), channel_id=1, replica_groups=mesh['row'=16,'col'=32] {'col'}, dimensions={0}, use_global_device_ids=true | all-gather | bytes 67584 | tf_op jit(solution)/shard_map/all_gather | solution.py:49
  146.7 23.6 %all-gather.1 = f32[32,64,4]{1,2,0:T(4,128)S(1)} all-gather(f32[1,64,4]{1,2,0:T(4,128)S(1)} %maximum_bitcast_fusion), channel_id=1, replica_groups=mesh['row'=16,'col'=32] {'col'}, dimensions={0}, use_global_device_ids=true | all-gather | bytes 33792 | tf_op jit(solution)/shard_map/all_gather | solution.py:39
  170.4 19.9 %all-gather.2 = f32[16,64,3]{1,2,0:T(4,128)S(1)} all-gather(f32[1,64,3]{1,2,0:T(4,128)S(1)} %bitcast.175), channel_id=1, replica_groups=mesh['row'=16,'col'=32] {'row'}, dimensions={0}, use_global_device_ids=true | all-gather | bytes 13056 | tf_op jit(solution)/shard_map/all_gather | solution.py:40
  190.4 4.5 while.34
  191.6 1.0 convolution_add_fusion.7
  196.0 59.8 %reduce-scatter.7.cloned.1.call-done = f32[64,16]{1,0:T(8,128)} async-done(((f32[1024,16]{1,0:T(8,128)}), f32[64,16]{1,0:T(8,128)}) %reduce-scatter.7.cloned.1.call-update) | async-done | bytes 4112
  256.7 111.7 %psum.43 = f32[16,16]{1,0:T(8,128)S(1)} all-reduce(f32[16,16]{1,0:T(8,128)S(1)} %fusion.46), channel_id=1, replica_groups=mesh['row'=16,'col'=32] {'row','col'}, use_global_device_ids=true, to_apply=%region_6.0 | all-reduce | flops 256 | bytes 2048 | tf_op jit(solution)/shard_map/psum | solution.py:28
  368.7 100.0 %psum.44 = f32[16,16]{0,1:T(8,128)S(1)} all-reduce(f32[16,16]{0,1:T(8,128)S(1)} %fusion.61), channel_id=1, replica_groups=mesh['row'=16,'col'=32] {'row','col'}, use_global_device_ids=true, to_apply=%region_7.0 | all-reduce | flops 256 | bytes 2048 | tf_op jit(solution)/shard_map/psum | solution.py:28
  468.8 1.5 cholesky.105
  471.6 1.2 custom-call.21
  473.2 24.4 %all-gather.3 = bf16[32,64,16]{1,2,0:T(8,128)(2,1)S(1)} all-gather(bf16[1,64,16]{1,2,0:T(8,128)(2,1)S(1)} %convert_bitcast_fusion), channel_id=1, replica_groups=mesh['row'=16,'col'=32] {'col'}, dimensions={0}, use_global_device_ids=true | all-gather | bytes 67584 | tf_op jit(solution)/shard_map/all_gather | solution.py:49
  497.7 4.5 while.35
  505.2 51.2 %reduce-scatter.9.cloned.1.call-done = f32[64,16]{1,0:T(8,128)} async-done(((f32[1024,16]{1,0:T(8,128)}), f32[64,16]{1,0:T(8,128)}) %reduce-scatter.9.cloned.1.call-update) | async-done | bytes 4112
  557.5 111.9 %all-reduce.2 = (f32[16,16]{1,0:T(8,128)S(1)}, f32[16,16]{1,0:T(8,128)S(1)}) all-reduce(f32[16,16]{1,0:T(8,128)S(1)} %fusion.54, f32[16,16]{1,0:T(8,128)S(1)} %fusion.53), channel_id=1, replica_groups=mesh['row'=16,'col'=32] {'row','col'}, use_global_device_ids=true, to_apply=%region_12.0 | all-reduce | flops 512 | bytes 4096 | tf_op jit(solution)/shard_map/psum | solution.py:28
  669.9 100.3 %psum.47 = f32[16,16]{0,1:T(8,128)S(1)} all-reduce(f32[16,16]{0,1:T(8,128)S(1)} %fusion.63), channel_id=1, replica_groups=mesh['row'=16,'col'=32] {'row','col'}, use_global_device_ids=true, to_apply=%region_14.0 | all-reduce | flops 256 | bytes 2048 | tf_op jit(solution)/shard_map/psum | solution.py:28
  770.3 1.5 cholesky.116
  773.3 2.0 dynamic-slice_select_fusion
  775.3 2.1 scatter.24
  779.3 2.9 cholesky.41
  783.5 2.4 custom-call.15
  786.7 1.2 custom-call.22
  (108 shorter events, 27.4 us)
Async XLA Ops:
  7.2 0.7 copy-start
  7.2 139.5 %copy-start.3 = (f32[64]{0:T(128)S(1)}, f32[64]{0:T(128)}, u32[]{:S(2)}) copy-start(f32[64]{0:T(128)} %param.24) | copy-start | bytes 772
  7.2 139.5 %copy-start.2 = (f32[3,64]{1,0:T(4,128)S(1)}, f32[3,64]{1,0:T(4,128)}, u32[]{:S(2)}) copy-start(f32[3,64]{1,0:T(4,128)} %param.23) | copy-start | bytes 2308
  7.2 248.6 %reduce-scatter.7.cloned.1.call-start = ((), (), s32[]{:S(2)}) async-start(), calls=%async_computation.2 | async-start | bytes 557056
  194.9 61.7 %copy-start.1 = (f32[64]{0:T(128)S(1)}, f32[64]{0:T(128)}, u32[]{:S(2)}) copy-start(f32[64]{0:T(128)} %param.25) | copy-start | bytes 772
  195.9 360.5 %reduce-scatter.9.cloned.1.call-start = ((), (), s32[]{:S(2)}) async-start(), calls=%async_computation.3 | async-start | bytes 557056
  502.3 1.6 copy-start.4
Sparse Core Ops, SparseCore 0:
  196.0 59.6 reduce-scatter.6
  503.4 52.9 reduce-scatter.8
where the time goes:
time: 798 us; the launch traced here: 797 us
  blocking collectives  626 us (78%)
  waiting for transfers between devices  111 us (14%)
  other arithmetic  22.3 us (3%)
  between operations  14.2 us (2%)
  matrix products  13.4 us (2%)
  local copies, waits for them, and re-layouts  10.1 us (1%)
    psum x5, blocking collectives, reduce_small(): return lax.psum(terms, ('row', 'col'))  535 us
    unnamed x4, waiting for transfers between devices  111 us
    all_gather x2, blocking collectives, body(): lax.all_gather(field.astype(jnp.bfloat16), 'col', axis=1, tiled=True)  47.3 us
    all_gather x1, blocking collectives, body(): sources = lax.all_gather(geom, 'col', axis=1, tiled=True)  23.6 us
    all_gather x1, blocking collectives, body(): targets = lax.all_gather(centroids, 'row', axis=1, tiled=True)  19.9 us
  transfers between devices with their start and end apart: 2, of which 2 were waited for; matrix products, arithmetic and copies ran while one was open for 0% of the time, Pallas kernels for 0%

commit v1 on v0

v1 whole, which is shorter than its diff:
```python
import math

import jax
import jax.numpy as jnp
from jax import lax
from jax.sharding import PartitionSpec as P

HIGH = lax.Precision.HIGHEST


def kernel_tile(src, tgt, scale, delta2):
    dx = src[0][:, None] - tgt[0][None, :]
    dy = src[1][:, None] - tgt[1][None, :]
    dz = src[2][:, None] - tgt[2][None, :]
    dist2 = dx * dx + dy * dy + dz * dz
    return (src[3][:, None] * scale * lax.rsqrt(dist2 + delta2)).astype(jnp.bfloat16)


def inner(left, right):
    return jnp.dot(left, right.T, precision=HIGH)


def lower_inverse(gram):
    factor = jnp.linalg.cholesky(gram)
    eye = jnp.eye(gram.shape[0], dtype=jnp.float32)
    return jax.scipy.linalg.solve_triangular(factor, eye, lower=True)


def spread(chunk, axis):
    size = lax.axis_size(axis)
    return lax.all_to_all(jnp.broadcast_to(chunk[None], (size,) + chunk.shape), axis, 0, 0)


def wide(parts):
    return parts.transpose(1, 0, 2).reshape(parts.shape[1], -1)


def body(centroids, areas, conductance, power):
    nrhs, width = power.shape
    rows, cols = lax.axis_size("row"), lax.axis_size("col")
    panels = width * rows * cols
    scale = 4.0 / (math.pi * panels)
    delta2 = 16.0 / panels
    cond_row = conductance[None, :]
    near = spread(jnp.concatenate([power, centroids, areas[None, :], cond_row], 0), "row")
    near = wide(near)
    power_near, sources = near[:nrhs], near[nrhs : nrhs + 4]
    gram0 = inner(power_near, power_near)
    mean = jnp.sum(near[nrhs + 4]) / panels
    pack = jnp.concatenate(
        [centroids.reshape(-1), gram0.reshape(-1), jnp.full((64,), mean)], 0
    ).reshape(-1, 128)
    far = spread(pack, "col").reshape(cols, -1)
    targets = wide(far[:, : 3 * width].reshape(cols, 3, width))
    total = jnp.sum(far[:, 3 * width :], 0)
    theta = total[nrhs * nrhs]
    inverse0 = lower_inverse(total[: nrhs * nrhs].reshape(nrhs, nrhs))
    v_near = jnp.dot(inverse0, power_near, precision=HIGH)
    v_own = jnp.dot(inverse0, power, precision=HIGH)
    tile = kernel_tile(sources, targets, scale, delta2)

    def scatter(partial):
        parts = partial.reshape(nrhs, cols, width).transpose(1, 0, 2)
        return jnp.sum(lax.all_to_all(parts, "col", 0, 0), 0)

    product = scatter(
        jnp.dot(v_near.astype(jnp.bfloat16), tile, preferred_element_type=jnp.float32)
    )
    w1 = cond_row * v_own + product
    u_near = wide(spread(w1, "row")) - theta * v_near
    u_own = w1 - theta * v_own
    high = u_near.astype(jnp.bfloat16)
    low = (u_near - high.astype(jnp.float32)).astype(jnp.bfloat16)
    both = jnp.dot(jnp.concatenate([high, low], 0), tile, preferred_element_type=jnp.float32)
    w2 = cond_row * u_own + scatter(both[:nrhs] + both[nrhs:])
    stack = jnp.concatenate([w1, w2, power], 0)
    gram = inner(stack[: 2 * nrhs], stack).reshape(-1, 128)
    gram = jnp.sum(spread(gram, "col"), 0)
    gram = jnp.sum(spread(gram, "row"), 0).reshape(2 * nrhs, 3 * nrhs)
    inverse = lower_inverse(gram[:, : 2 * nrhs])
    coeff = jnp.dot(
        inverse.T, jnp.dot(inverse, gram[:, 2 * nrhs :], precision=HIGH), precision=HIGH
    )
    basis = jnp.concatenate([v_own, u_own], 0)
    solution = jnp.dot(coeff.T, basis, precision=HIGH)
    residual = power - jnp.dot(coeff.T, stack[: 2 * nrhs], precision=HIGH)
    return (solution, residual)


def solution(mesh):
    return jax.shard_map(
        body,
        mesh=mesh,
        in_specs=(
            P(None, ("col", "row")),
            P(("col", "row")),
            P(("col", "row")),
            P(None, ("col", "row")),
        ),
        out_specs=(P(None, ("col", "row")), P(None, ("col", "row"))),
        check_vma=False,
    )
```

time: 798 us -> 147 us (0.18)
  blocking collectives: 626 us -> 51.1 us
  waiting for transfers between devices: 111 us -> 29.7 us
  starting transfers between devices: 0.08 us -> 28.8 us
  between operations: 14.2 us -> 1.58 us
    psum x5 -> x0, blocking collectives: 535 us -> none  [reduce_small(): return lax.psum(terms, ('row', 'col'))]
    unnamed x4 -> x0, waiting for transfers between devices: 111 us -> none
    all_gather x4 -> x0, blocking collectives: 90.8 us -> none  [the longest x2 47.3 us: body(): lax.all_gather(field.astype(jnp.bfloat16), 'col', axis=1, tiled=True)]
    all_to_all x0 -> x4, blocking collectives: none -> 51.1 us  [the longest x2 27.2 us: spread(): lax.all_to_all(jnp.broadcast_to(chunk[None], (size,) + chunk.shape), axis...]
    all_to_all x0 -> x3, waiting for transfers between devices: none -> 29.7 us  [spread(): lax.all_to_all(jnp.broadcast_to(chunk[None], (size,) + chunk.shape), axis...]
    all_to_all x0 -> x3, starting transfers between devices: none -> 28.8 us  [spread(): lax.all_to_all(jnp.broadcast_to(chunk[None], (size,) + chunk.shape), axis...]
    another operation x14 -> x4, other arithmetic: 15.1 us -> 4.96 us  [lower_inverse(): return jax.scipy.linalg.solve_triangular(factor, eye, lower=True)]
  transfers between devices with their start and end apart: 2 -> 3, of which waited for: 2 -> 3; matrix products, arithmetic and copies ran while one was open for 0% -> 1% of each run, Pallas kernels for 0% -> 0%
where the time goes in v1:
time: 147 us; the launch traced here: 145 us
  blocking collectives  51.1 us (35%)
  waiting for transfers between devices  29.7 us (20%)
  starting transfers between devices  28.8 us (20%)
  other arithmetic  17.4 us (12%)
  matrix products  9.74 us (7%)
  local copies, waits for them, and re-layouts  6.63 us (5%)
  between operations  1.58 us (1%)
    all_to_all x3, waiting for transfers between devices, spread(): lax.all_to_all(jnp.broadcast_to(chunk[None], (size,) + chunk.shape), axis...  29.7 us
    all_to_all x3, starting transfers between devices, spread(): lax.all_to_all(jnp.broadcast_to(chunk[None], (size,) + chunk.shape), axis...  28.8 us
    all_to_all x2, blocking collectives, spread(): lax.all_to_all(jnp.broadcast_to(chunk[None], (size,) + chunk.shape), axis...  27.2 us
    all_to_all x2, blocking collectives, scatter(): return jnp.sum(lax.all_to_all(parts, 'col', 0, 0), 0)  24 us
    another operation x6, other arithmetic, lower_inverse(): factor = jnp.linalg.cholesky(gram)  5.73 us
    another operation x4, other arithmetic, lower_inverse(): return jax.scipy.linalg.solve_triangular(factor, eye, lower=True)  4.96 us
    dot_general x1, matrix products, body(): jnp.dot(jnp.concatenate([high, low], 0), tile, preferred_element_type=jnp...  3.42 us
    dot_general x1, matrix products, body(): jnp.dot(v_near.astype(jnp.bfloat16), tile, preferred_element_type=jnp.flo...  3.3 us
  transfers between devices with their start and end apart: 3, of which 3 were waited for; matrix products, arithmetic and copies ran while one was open for 1% of the time, Pallas kernels for 0%

profile of v1, /device:TPU:1, one launch (start us, length us, event | category | flops | bytes accessed | tf_op | source)
XLA Modules:
  0.0 145.0 jit_solution(11072213371408586244)
XLA Ops:
  0.6 0.8 pad_maximum_fusion.3
  1.4 0.8 reshape.143
  2.2 15.7 %all-to-all-start = ((f32[16,1,1344]{2,1,0:T(1,128)}), f32[16,1,1344]{2,1,0:T(1,128)S(1)}, u32[]{:S(2)}, u32[]{:S(2)}) async-start(f32[16,1,1344]{2,1,0:T(1,128)} %reshape.143), calls=%async_computation | async-start | bytes 180224 | tf_op jit(solution)/shard_map/all_to_all | solution.py:31
  18.0 11.7 %all-to-all-done = f32[16,1,1344]{2,1,0:T(1,128)S(1)} async-done(((f32[16,1,1344]{2,1,0:T(1,128)}), f32[16,1,1344]{2,1,0:T(1,128)S(1)}, u32[]{:S(2)}, u32[]{:S(2)}) %all-to-all-start) | async-done | bytes 86048 | tf_op jit(solution)/shard_map/all_to_all | solution.py:31
  30.2 0.9 reduce.41
  31.4 0.8 fusion.24
  33.7 9.6 %all-to-all-start.1 = ((f32[32,4,128]{2,1,0:T(4,128)}), f32[32,4,128]{2,1,0:T(4,128)S(1)}, u32[]{:S(2)}, u32[]{:S(2)}) async-start(f32[32,4,128]{2,1,0:T(4,128)} %broadcast_in_dim.50), calls=%async_computation.1 | async-start | bytes 131072 | tf_op jit(solution)/shard_map/all_to_all | solution.py:31
  43.7 6.9 %all-to-all-done.1 = f32[32,4,128]{2,1,0:T(4,128)S(1)} async-done(((f32[32,4,128]{2,1,0:T(4,128)}), f32[32,4,128]{2,1,0:T(4,128)S(1)}, u32[]{:S(2)}, u32[]{:S(2)}) %all-to-all-start.1) | async-done | bytes 65568 | tf_op jit(solution)/shard_map/all_to_all | solution.py:31
  50.9 1.5 %cholesky.34 = f32[16,16]{1,0:T(8,128)S(1)} custom-call(f32[16,16]{1,0:T(8,128)S(1)} %fusion.27), custom_call_target="Cholesky" | custom-call | tf_op jit(solution)/shard_map/jit(cholesky)/cholesky | solution.py:24
  53.7 1.2 custom-call.14
  55.7 3.3 %fusion.1 = f32[16,2048]{1,0:T(8,128)S(1)} fusion(f32[2048]{0:T(1024)S(1)} %sub.75, f32[1024]{0:T(1024)S(1)} %sub.73, f32[2048]{0:T(1024)S(1)} %sub.70, f32[1024]{0:T(1024)S(1)} %sub.68, f32[2048]{0:T(1024)S(1)} %sub.65, f32[1024]{0:T(1024)S(1)} %sub.63, f32[1024]{0:T(1024)S(1)} %mul.61, f32[16,1024]{1,0:T(8,128)S(1)} %fusion.35), kind=kOutput, calls=%fused_computation.2 | convolution fusion | flops 90193920 | bytes 237568 | tf_op jit(solution)/shard_map/dot_general | solution.py:67
  59.5 11.2 %all_to_all.35 = f32[32,1,1024]{2,1,0:T(1,128)S(1)} all-to-all(f32[32,1,1024]{2,1,0:T(1,128)S(1)} %reshape.145), channel_id=1, replica_groups=mesh['row'=16,'col'=32] {'col'}, dimensions={0} | all-to-all | bytes 262144 | tf_op jit(solution)/shard_map/all_to_all | solution.py:64
  70.7 1.0 reduce.42
  73.2 3.5 %all-to-all-start.3 = ((f32[16,1,1024]{2,1,0:T(1,128)}), f32[16,1,1024]{2,1,0:T(1,128)S(1)}, u32[]{:S(2)}, u32[]{:S(2)}) async-start(f32[16,1,1024]{2,1,0:T(1,128)} %reshape.147), calls=%async_computation.3 | async-start | bytes 131072 | tf_op jit(solution)/shard_map/all_to_all | solution.py:31
  77.3 11.1 %all-to-all-done.3 = f32[16,1,1024]{2,1,0:T(1,128)S(1)} async-done(((f32[16,1,1024]{2,1,0:T(1,128)}), f32[16,1,1024]{2,1,0:T(1,128)S(1)}, u32[]{:S(2)}, u32[]{:S(2)}) %all-to-all-start.3) | async-done | bytes 65568 | tf_op jit(solution)/shard_map/all_to_all | solution.py:31
  88.4 0.8 reduce.43
  90.1 3.4 %fusion = f32[32,2048]{1,0:T(8,128)S(1)} fusion(f32[2048]{0:T(1024)S(1)} %sub.75, f32[1024]{0:T(1024)S(1)} %sub.73, f32[2048]{0:T(1024)S(1)} %sub.70, f32[1024]{0:T(1024)S(1)} %sub.68, f32[2048]{0:T(1024)S(1)} %sub.65, f32[1024]{0:T(1024)S(1)} %sub.63, f32[1024]{0:T(1024)S(1)} %mul.61, bf16[16,1024]{1,0:T(8,128)(2,1)S(1)} %get-tuple-element.13, ...), kind=kOutput, calls=%fused_computation.1 | convolution fusion | flops 157417472 | bytes 368640 | tf_op jit(solution)/shard_map/dot_general | solution.py:74
  94.0 12.8 %all_to_all.36 = f32[32,1,1024]{2,1,0:T(1,128)S(1)} all-to-all(f32[32,1,1024]{2,1,0:T(1,128)S(1)} %reshape.149), channel_id=1, replica_groups=mesh['row'=16,'col'=32] {'col'}, dimensions={0} | all-to-all | bytes 262144 | tf_op jit(solution)/shard_map/all_to_all | solution.py:64
  106.8 1.0 reduce.44
  108.8 12.5 %all_to_all.37 = f32[32,12,128]{2,1,0:T(8,128)S(1)} all-to-all(f32[32,12,128]{2,1,0:T(8,128)S(1)} %broadcast_in_dim.53), channel_id=1, replica_groups=mesh['row'=16,'col'=32] {'col'}, dimensions={0} | all-to-all | bytes 393216 | tf_op jit(solution)/shard_map/all_to_all | solution.py:31
  121.4 14.6 %all_to_all.38 = f32[16,12,128]{2,1,0:T(8,128)S(1)} all-to-all(f32[16,12,128]{2,1,0:T(8,128)S(1)} %broadcast_in_dim.54), channel_id=1, replica_groups=mesh['row'=16,'col'=32] {'row'}, dimensions={0} | all-to-all | bytes 196608 | tf_op jit(solution)/shard_map/all_to_all | solution.py:31
  136.2 2.9 %cholesky.65 = f32[32,32]{1,0:T(8,128)S(1)} custom-call(f32[32,32]{1,0:T(8,128)S(1)} %fusion.22), custom_call_target="Cholesky" | custom-call | tf_op jit(solution)/shard_map/jit(cholesky)/cholesky | solution.py:24
  140.5 2.4 %custom-call.15 = f32[1,32,32]{1,2,0:T(8,128)S(1)} custom-call(f32[1,32,32]{2,1,0:T(8,128)S(1)} %fusion.13), custom_call_target="InvertDiagBlocksLowerTriangular" | custom-call | tf_op jit(solution)/shard_map/jit(_solve_triangular)/triangular_solve | solution.py:26
  143.6 0.7 convolution_subtract_fusion
  (75 shorter events, 12.4 us)
Async XLA Ops:
  1.4 16.5 %copy-start.1 = (f32[3,64]{1,0:T(4,128)S(1)}, f32[3,64]{1,0:T(4,128)}, u32[]{:S(2)}) copy-start(f32[3,64]{1,0:T(4,128)} %param.4) | copy-start | bytes 2308
  2.2 27.5 %all-to-all-start = ((f32[16,1,1344]{2,1,0:T(1,128)}), f32[16,1,1344]{2,1,0:T(1,128)S(1)}, u32[]{:S(2)}, u32[]{:S(2)}) async-start(f32[16,1,1344]{2,1,0:T(1,128)} %reshape.143), calls=%async_computation | async-start | bytes 180224 | tf_op jit(solution)/shard_map/all_to_all | solution.py:31
  33.7 16.9 %all-to-all-start.1 = ((f32[32,4,128]{2,1,0:T(4,128)}), f32[32,4,128]{2,1,0:T(4,128)S(1)}, u32[]{:S(2)}, u32[]{:S(2)}) async-start(f32[32,4,128]{2,1,0:T(4,128)} %broadcast_in_dim.50), calls=%async_computation.1 | async-start | bytes 131072 | tf_op jit(solution)/shard_map/all_to_all | solution.py:31
  71.6 0.7 copy-start
  71.6 0.7 copy-start.2
  73.2 15.1 %all-to-all-start.3 = ((f32[16,1,1024]{2,1,0:T(1,128)}), f32[16,1,1024]{2,1,0:T(1,128)S(1)}, u32[]{:S(2)}, u32[]{:S(2)}) async-start(f32[16,1,1024]{2,1,0:T(1,128)} %reshape.147), calls=%async_computation.3 | async-start | bytes 131072 | tf_op jit(solution)/shard_map/all_to_all | solution.py:31

commit v2 on v1

v2 whole, which is shorter than its diff:
```python
import functools
import math

import jax
import jax.numpy as jnp
from jax import lax
from jax.experimental import pallas as pl
from jax.experimental.pallas import tpu as pltpu
from jax.sharding import PartitionSpec as P

HIGH = lax.Precision.HIGHEST
F32 = jnp.float32
BF16 = jnp.bfloat16


def mm(a, b):
    return jnp.dot(a, b, precision=HIGH, preferred_element_type=F32)


def mm_t(a, b):
    return lax.dot_general(
        a, b, (((1,), (1,)), ((), ())), precision=HIGH, preferred_element_type=F32
    )


def t_mm(a, b):
    return lax.dot_general(
        a, b, (((0,), (0,)), ((), ())), precision=HIGH, preferred_element_type=F32
    )


def call(fn, outs, *args, scratch=()):
    vmem = pl.BlockSpec(memory_space=pltpu.VMEM)
    return pl.pallas_call(
        fn,
        out_shape=tuple(jax.ShapeDtypeStruct(shape, dtype) for shape, dtype in outs),
        in_specs=[vmem] * len(args),
        out_specs=tuple(vmem for _ in outs),
        scratch_shapes=list(scratch),
        compiler_params=pltpu.CompilerParams(vmem_limit_bytes=32 * 1024 * 1024),
    )(*args)


def forward(gram, right):
    n = gram.shape[0]
    a = jnp.concatenate([gram, right], 1)
    row_id = lax.broadcasted_iota(jnp.int32, (n, 1), 0)
    scale = jnp.zeros((n, 1), F32)
    for k in range(n):
        pivot = a[k : k + 1, k : k + 1]
        col = a[:, k : k + 1] * (1.0 / pivot)
        scale = jnp.where(row_id == k, lax.rsqrt(pivot), scale)
        a = a - jnp.where(row_id > k, col, 0.0) * a[k : k + 1, :]
    return a[:, n:] * scale


def identity(n):
    return (
        lax.broadcasted_iota(jnp.int32, (n, n), 0) == lax.broadcasted_iota(jnp.int32, (n, n), 1)
    ).astype(F32)


def solve(gram, right):
    n = gram.shape[0]
    a = jnp.concatenate([gram, right], 1)
    row_id = lax.broadcasted_iota(jnp.int32, (n, 1), 0)
    for k in range(n):
        inv = 1.0 / a[k : k + 1, k : k + 1]
        pivot_row = a[k : k + 1, :] * inv
        col = jnp.where(row_id == k, 0.0, a[:, k : k + 1])
        a = jnp.where(row_id == k, pivot_row, a - col * pivot_row)
    return a[:, n:]


def spread_out(ref, chunk):
    for i in range(ref.shape[0]):
        ref[i] = chunk


def tree_sum(ref):
    parts = [ref[i] for i in range(ref.shape[0])]
    while len(parts) > 1:
        parts = [parts[i] + parts[i + 1] for i in range(0, len(parts), 2)]
    return parts[0]


def left_pairs(ref, rows):
    return jnp.concatenate([ref[i, rows, :64] for i in range(ref.shape[0])], 1)


def pack_kernel(cen, area, cond, power, out, tmp):
    tmp[...] = jnp.zeros_like(tmp)
    tmp[:, :64] = power[...]
    tmp[0:3, 64:] = cen[...]
    tmp[3:4, 64:] = area[...]
    tmp[4:5, 64:] = cond[...]
    spread_out(out, tmp[...])


def near_kernel(scale, near, cen, out, power_near, src, tmp):
    p = jnp.concatenate([near[i, :, :64] for i in range(near.shape[0])], 1)
    g = jnp.concatenate([near[i, 0:8, 64:] for i in range(near.shape[0])], 1)
    power_near[...] = p
    row_id = lax.broadcasted_iota(jnp.int32, g.shape, 0)
    src[...] = jnp.where(row_id == 3, g * scale, g)
    gram = mm_t(p, p)
    tmp[...] = jnp.zeros_like(tmp)
    tmp[0:3, :64] = cen[...]
    tmp[3:4, :64] = jnp.broadcast_to(jnp.sum(g[4:5, :], 1, keepdims=True), (1, 64))
    tmp[:, 64:80] = gram[:8]
    tmp[:, 80:96] = gram[8:]
    spread_out(out, tmp[...])


def first_kernel(panels, far, power_near, power, tgt, v_near, v_bf, v_own, theta):
    tgt[...] = jnp.concatenate([far[i, :, :64] for i in range(far.shape[0])], 1)
    total = tree_sum(far)
    gram = jnp.concatenate([total[:, 64:80], total[:, 80:96]], 0)
    theta[...] = jnp.broadcast_to(total[3:4, 0:1] * (1.0 / panels), theta.shape)
    inverse = forward(gram, identity(gram.shape[0]))
    v = mm(inverse, power_near[...])
    v_near[...] = v
    v_bf[...] = v.astype(BF16)
    v_own[...] = mm(inverse, power[...])


def second_kernel(recv, cond, v_own, theta, out, w_own, u_own, tmp):
    total = tree_sum(recv)
    product = jnp.concatenate([total[:, :64], total[:, 64:]], 0)
    w = cond[...] * v_own[...] + product
    u = w - theta[0:1, 0:64] * v_own[...]
    w_own[...] = w
    u_own[...] = u
    tmp[:, :64] = u
    tmp[:, 64:] = jnp.zeros_like(u)
    spread_out(out, tmp[...])


def third_kernel(recv, v_near, u_split, gram):
    u = jnp.concatenate([recv[i, :, :64] for i in range(recv.shape[0])], 1)
    high = u.astype(BF16)
    u_split[0:16] = high
    u_split[16:32] = (u - high.astype(F32)).astype(BF16)
    gram[...] = jnp.concatenate([mm_t(v_near[...], u), mm_t(u, u)], 1)


def fourth_kernel(partial, gram, out):
    both = partial[0:16] + partial[16:32]
    extra = jnp.concatenate([gram[...], jnp.zeros((16, 32), F32)], 1)
    for i in range(out.shape[0]):
        out[i, :, :64] = both[:, i * 64 : i * 64 + 64]
        out[i, :, 64:] = extra


def fifth_kernel(recv, cond, v_own, w_own, u_own, power, out, basis, images, tmp):
    total = tree_sum(recv)
    shifted = total[:, 64:80]
    gram = total[:, 80:96]
    v, w, u = v_own[...], w_own[...], u_own[...]
    x = cond[...] * u + total[:, :64]
    both = jnp.concatenate([x, u], 1) - t_mm(shifted, jnp.concatenate([w, v], 1))
    both = forward(gram - t_mm(shifted, shifted), both)
    images[0:16] = w
    images[16:32] = both[:, :64]
    basis[0:16] = v
    basis[16:32] = both[:, 64:]
    stack = jnp.concatenate([images[...], power[...]], 0)
    small = mm_t(images[...], stack)
    tmp[...] = jnp.zeros_like(tmp)
    tmp[:, 0:48] = small[:16]
    tmp[:, 64:112] = small[16:]
    spread_out(out, tmp[...])


def sixth_kernel(recv, out):
    spread_out(out, tree_sum(recv))


def last_kernel(recv, basis, images, power, sol, res):
    total = tree_sum(recv)
    system = jnp.concatenate([total[:, 0:48], total[:, 64:112]], 0)
    coeff = solve(system[:, :32], system[:, 32:])
    sol[...] = t_mm(coeff, basis[...])
    res[...] = power[...] - t_mm(coeff, images[...])


def kernel_tile(src, tgt, delta2):
    dx = src[0][:, None] - tgt[0][None, :]
    dy = src[1][:, None] - tgt[1][None, :]
    dz = src[2][:, None] - tgt[2][None, :]
    dist2 = dx * dx + dy * dy + dz * dz
    return (src[3][:, None] * lax.rsqrt(dist2 + delta2)).astype(BF16)


def exchange(parts, axis):
    return lax.all_to_all(parts, axis, 0, 0)


def body(centroids, areas, conductance, power):
    nrhs, width = power.shape
    rows, cols = lax.axis_size("row"), lax.axis_size("col")
    panels = width * rows * cols
    scale = 4.0 / (math.pi * panels)
    delta2 = 16.0 / panels
    area, cond = areas[None, :], conductance[None, :]
    n_near, n_far = width * rows, width * cols
    (chunk,) = call(
        pack_kernel, [((rows, 16, 128), F32)], centroids, area, cond, power,
        scratch=[pltpu.VMEM((16, 128), F32)],
    )
    near = exchange(chunk, "row")
    chunk, power_near, src = call(
        functools.partial(near_kernel, scale),
        [((cols, 8, 128), F32), ((16, n_near), F32), ((8, n_near), F32)],
        near, centroids,
        scratch=[pltpu.VMEM((8, 128), F32)],
    )
    far = exchange(chunk, "col")
    tgt, v_near, v_bf, v_own, theta = call(
        functools.partial(first_kernel, panels),
        [((8, n_far), F32), ((16, n_near), F32), ((16, n_near), BF16), ((16, width), F32), ((1, 128), F32)],
        far, power_near, power,
    )
    tile = kernel_tile(src, tgt, delta2)
    partial = jnp.dot(v_bf, tile, preferred_element_type=F32)
    parts = partial.reshape(2, 8, cols, width).transpose(2, 1, 0, 3).reshape(cols, 8, 128)
    recv = exchange(parts, "col")
    chunk, w_own, u_own = call(
        second_kernel, [((rows, 16, 128), F32), ((16, width), F32), ((16, width), F32)],
        recv, cond, v_own, theta,
        scratch=[pltpu.VMEM((16, 128), F32)],
    )
    recv = exchange(chunk, "row")
    u_split, gram = call(
        third_kernel, [((32, n_near), BF16), ((16, 32), F32)], recv, v_near
    )
    partial = jnp.dot(u_split, tile, preferred_element_type=F32)
    (parts,) = call(fourth_kernel, [((cols, 16, 128), F32)], partial, gram)
    recv = exchange(parts, "col")
    chunk, basis, images = call(
        fifth_kernel,
        [((cols, 16, 128), F32), ((32, width), F32), ((32, width), F32)],
        recv, cond, v_own, w_own, u_own, power,
        scratch=[pltpu.VMEM((16, 128), F32)],
    )
    recv = exchange(chunk, "col")
    (chunk,) = call(sixth_kernel, [((rows, 16, 128), F32)], recv)
    recv = exchange(chunk, "row")
    return call(
        last_kernel, [((16, width), F32), ((16, width), F32)], recv, basis, images, power
    )


def solution(mesh):
    return jax.shard_map(
        body,
        mesh=mesh,
        in_specs=(
            P(None, ("col", "row")),
            P(("col", "row")),
            P(("col", "row")),
            P(None, ("col", "row")),
        ),
        out_specs=(P(None, ("col", "row")), P(None, ("col", "row"))),
        check_vma=False,
    )
```

time: 147 us -> 137 us (0.932)
  blocking collectives: 51.1 us -> 97.8 us
  waiting for transfers between devices: 29.7 us -> 7.61 us
  starting transfers between devices: 28.8 us -> 10.7 us
  other arithmetic: 17.4 us -> 0 us
  Pallas kernels: 0 us -> 9.06 us
  local copies, waits for them, and re-layouts: 6.63 us -> 3.22 us
  matrix products: 9.74 us -> 6.83 us
    all_to_all x4 -> x6, blocking collectives: 51.1 us -> 97.8 us  [exchange(): return lax.all_to_all(parts, axis, 0, 0)]
    all_to_all x3 -> x1, waiting for transfers between devices: 29.7 us -> 7.61 us  [exchange(): return lax.all_to_all(parts, axis, 0, 0)]
    all_to_all x3 -> x1, starting transfers between devices: 28.8 us -> 10.7 us  [exchange(): return lax.all_to_all(parts, axis, 0, 0)]
    another operation x10 -> x0, other arithmetic: 10.7 us -> none  [the longest x6 5.73 us: lower_inverse(): factor = jnp.linalg.cholesky(gram)]
    pallas_call x0 -> x9, Pallas kernels: none -> 9.06 us  [call(): pl.pallas_call(fn, out_shape=tuple((jax.ShapeDtypeStruct(shape, dtype) fo...]
    all_to_all x4 -> x0, other arithmetic: 3.55 us -> none  [the longest x2 1.9 us: scatter(): return jnp.sum(lax.all_to_all(parts, 'col', 0, 0), 0)]
    dot_general x10 -> x2, matrix products: 9.33 us -> 6.83 us  [the longest x1 3.51 us: body(): partial = jnp.dot(u_split, tile, preferred_element_type=F32)]
  transfers between devices with their start and end apart: 3 -> 1, of which waited for: 3 -> 1; matrix products, arithmetic and copies ran while one was open for 1% -> 0% of each run, Pallas kernels for 0% -> 0%
where the time goes in v2:
time: 137 us; the launch traced here: 136 us
  blocking collectives  97.8 us (71%)
  starting transfers between devices  10.7 us (8%)
  Pallas kernels  9.06 us (7%)
  waiting for transfers between devices  7.61 us (6%)
  matrix products  6.83 us (5%)
  local copies, waits for them, and re-layouts  3.22 us (2%)
    all_to_all x6, blocking collectives, exchange(): return lax.all_to_all(parts, axis, 0, 0)  97.8 us
    all_to_all x1, starting transfers between devices, exchange(): return lax.all_to_all(parts, axis, 0, 0)  10.7 us
    pallas_call x9, Pallas kernels, call(): pl.pallas_call(fn, out_shape=tuple((jax.ShapeDtypeStruct(shape, dtype) fo...  9.06 us
    all_to_all x1, waiting for transfers between devices, exchange(): return lax.all_to_all(parts, axis, 0, 0)  7.61 us
    dot_general x1, matrix products, body(): partial = jnp.dot(u_split, tile, preferred_element_type=F32)  3.51 us
    dot_general x1, matrix products, body(): partial = jnp.dot(v_bf, tile, preferred_element_type=F32)  3.32 us
  transfers between devices with their start and end apart: 1, of which 1 were waited for; matrix products, arithmetic and copies ran while one was open for 0% of the time, Pallas kernels for 0%

profile of v2, /device:TPU:1, one launch (start us, length us, event | category | flops | bytes accessed | tf_op | source)
XLA Modules:
  0.0 136.0 jit_solution(1540928056349285721)
XLA Ops:
  0.6 0.7 copy-done
  1.3 0.7 copy-done.2
  2.0 0.7 copy-done.3
  2.7 0.7 copy-done.5
  3.4 27.5 %all_to_all.35.near = f32[16,16,128]{2,1,0:T(8,128)S(1)} all-to-all(f32[16,16,128]{2,1,0:T(8,128)S(1)} %shard_map.59), channel_id=1, replica_groups=mesh['row'=16,'col'=32] {'row'}, dimensions={0} | all-to-all | bytes 262144 | tf_op jit(solution)/shard_map/all_to_all | solution.py:196
  30.9 1.0 shard_map.60
  32.0 10.7 %all-to-all-start.1 = ((f32[32,8,128]{2,1,0:T(8,128)}), f32[32,8,128]{2,1,0:T(8,128)S(1)}, u32[]{:S(2)}, u32[]{:S(2)}) async-start(f32[32,8,128]{2,1,0:T(8,128)} %get-tuple-element.18), calls=%async_computation.1 | async-start | bytes 262144 | tf_op jit(solution)/shard_map/all_to_all | solution.py:196
  42.7 7.6 %all-to-all-done.1.far = f32[32,8,128]{2,1,0:T(8,128)S(1)} async-done(((f32[32,8,128]{2,1,0:T(8,128)}), f32[32,8,128]{2,1,0:T(8,128)S(1)}, u32[]{:S(2)}, u32[]{:S(2)}) %all-to-all-start.1) | async-done | bytes 131104 | tf_op jit(solution)/shard_map/all_to_all | solution.py:196
  50.3 1.7 %shard_map.61 = (f32[8,2048]{1,0:T(8,128)S(1)}, f32[16,1024]{1,0:T(8,128)S(1)}, bf16[16,1024]{1,0:T(8,128)(2,1)S(1)}, f32[16,64]{1,0:T(8,128)S(1)}, f32[1,128]{1,0:T(1,128)S(1)}) custom-call(f32[32,8,128]{2,1,0:T(8,128)S(1)} %all-to-all-done.1.far, f32[16,1024]{1,0:T(8,128)S(1)} %get-tuple-element.19.power_near, f32[16,64]{1,0:T(8,128)S(1)} %copy-done.1), custom_call_target="tpu_custom_call" | custom-call | tf_op jit(solution)/shard_map/pallas_call | solution.py:34
  52.1 3.3 %fusion.1 = f32[16,2048]{1,0:T(8,128)S(1)} fusion(bf16[16,1024]{1,0:T(8,128)(2,1)S(1)} %get-tuple-element.20, f32[2048]{0:T(1024)S(1)} %bitcast.21, f32[1024]{0:T(1024)S(1)} %bitcast.27, f32[2048]{0:T(1024)S(1)} %bitcast.23, f32[1024]{0:T(1024)S(1)} %bitcast.29, f32[2048]{0:T(1024)S(1)} %bitcast.19, f32[1024]{0:T(1024)S(1)} %bitcast.31, f32[1024]{0:T(1024)S(1)} %bitcast.25), kind=kOutput, calls=%fused_computation.2 | convolution fusion | flops 90177536 | bytes 204800 | tf_op jit(solution)/shard_map/dot_general | solution.py:225
  55.4 0.1 reshape.14
  55.5 0.2 copy.8
  55.7 0.2 reshape.15
  55.9 11.3 %all_to_all.36.recv = f32[32,8,128]{2,1,0:T(8,128)S(1)} all-to-all(f32[32,8,128]{2,1,0:T(8,128)S(1)} %reshape.15), channel_id=1, replica_groups=mesh['row'=16,'col'=32] {'col'}, dimensions={0} | all-to-all | bytes 262144 | tf_op jit(solution)/shard_map/all_to_all | solution.py:196
  67.2 0.1 shard_map.62
  67.3 15.5 %all_to_all.37.recv = f32[16,16,128]{2,1,0:T(8,128)S(1)} all-to-all(f32[16,16,128]{2,1,0:T(8,128)S(1)} %get-tuple-element.25), channel_id=1, replica_groups=mesh['row'=16,'col'=32] {'row'}, dimensions={0} | all-to-all | bytes 262144 | tf_op jit(solution)/shard_map/all_to_all | solution.py:196
  82.7 0.4 shard_map.63
  83.1 3.5 %fusion.partial = f32[32,2048]{1,0:T(8,128)S(1)} fusion(bf16[32,1024]{1,0:T(8,128)(2,1)S(1)} %get-tuple-element.27, f32[2048]{0:T(1024)S(1)} %bitcast.22, f32[1024]{0:T(1024)S(1)} %bitcast.28, f32[2048]{0:T(1024)S(1)} %bitcast.24, f32[1024]{0:T(1024)S(1)} %bitcast.30, f32[2048]{0:T(1024)S(1)} %bitcast.20, f32[1024]{0:T(1024)S(1)} %bitcast.32, ...), kind=kOutput, calls=%fused_computation.1 | convolution fusion | flops 157286400 | bytes 368640 | tf_op jit(solution)/shard_map/dot_general | solution.py:237
  86.6 0.1 shard_map.64
  86.7 15.3 %all_to_all.38.recv = f32[32,16,128]{2,1,0:T(8,128)S(1)} all-to-all(f32[32,16,128]{2,1,0:T(8,128)S(1)} %shard_map.64), channel_id=1, replica_groups=mesh['row'=16,'col'=32] {'col'}, dimensions={0} | all-to-all | bytes 524288 | tf_op jit(solution)/shard_map/all_to_all | solution.py:196
  102.0 2.1 %shard_map.65 = (f32[32,16,128]{2,1,0:T(8,128)S(1)}, f32[32,64]{1,0:T(8,128)S(1)}, f32[32,64]{1,0:T(8,128)S(1)}) custom-call(f32[32,16,128]{2,1,0:T(8,128)S(1)} %all_to_all.38.recv, f32[1,64]{1,0:T(1,128)S(1)} %bitcast.16, f32[16,64]{1,0:T(8,128)S(1)} %get-tuple-element.23.v_own, f32[16,64]{1,0:T(8,128)S(1)} %get-tuple-element.29.w_own, ...), custom_call_target="tpu_custom_call" | custom-call | tf_op jit(solution)/shard_map/pallas_call | solution.py:34
  104.1 12.5 %all_to_all.39.recv = f32[32,16,128]{2,1,0:T(8,128)S(1)} all-to-all(f32[32,16,128]{2,1,0:T(8,128)S(1)} %get-tuple-element.31), channel_id=1, replica_groups=mesh['row'=16,'col'=32] {'col'}, dimensions={0} | all-to-all | bytes 524288 | tf_op jit(solution)/shard_map/all_to_all | solution.py:196
  116.6 15.8 %all_to_all.40.recv = f32[16,16,128]{2,1,0:T(8,128)S(1)} all-to-all(f32[16,16,128]{2,1,0:T(8,128)S(1)} %shard_map.66), channel_id=1, replica_groups=mesh['row'=16,'col'=32] {'row'}, dimensions={0} | all-to-all | bytes 262144 | tf_op jit(solution)/shard_map/all_to_all | solution.py:196
  132.4 3.6 %shard_map.67 = (f32[16,64]{1,0:T(8,128)}, f32[16,64]{1,0:T(8,128)}) custom-call(f32[16,16,128]{2,1,0:T(8,128)S(1)} %all_to_all.40.recv, f32[32,64]{1,0:T(8,128)S(1)} %get-tuple-element.32.basis, f32[32,64]{1,0:T(8,128)S(1)} %get-tuple-element.33.images, f32[16,64]{1,0:T(8,128)S(1)} %copy-done.1), custom_call_target="tpu_custom_call" | custom-call | tf_op jit(solution)/shard_map/pallas_call | solution.py:34
  (12 shorter events, 0.2 us)
Async XLA Ops:
  0.6 0.7 copy-start
  1.3 0.7 copy-start.2
  2.0 0.7 copy-start.3
  2.7 0.7 copy-start.5
  30.9 19.4 %copy-start.1 = (f32[16,64]{1,0:T(8,128)S(1)}, f32[16,64]{1,0:T(8,128)}, u32[]{:S(2)}) copy-start(f32[16,64]{1,0:T(8,128)} %power.7) | copy-start | bytes 12292
  32.0 18.4 %all-to-all-start.1 = ((f32[32,8,128]{2,1,0:T(8,128)}), f32[32,8,128]{2,1,0:T(8,128)S(1)}, u32[]{:S(2)}, u32[]{:S(2)}) async-start(f32[32,8,128]{2,1,0:T(8,128)} %get-tuple-element.18), calls=%async_computation.1 | async-start | bytes 262144 | tf_op jit(solution)/shard_map/all_to_all | solution.py:196
  55.7 11.5 %copy-start.4 = (f32[64]{0:T(128)S(1)}, f32[64]{0:T(128)}, u32[]{:S(2)}) copy-start(f32[64]{0:T(128)} %param.6) | copy-start | bytes 772

commit v3 on v1

v3 whole, which is shorter than its diff:
```python
import functools
import math

import jax
import jax.numpy as jnp
from jax import lax
from jax.experimental import pallas as pl
from jax.experimental.pallas import tpu as pltpu
from jax.sharding import PartitionSpec as P

HIGH = lax.Precision.HIGHEST
F32 = jnp.float32
BF16 = jnp.bfloat16


def mm(a, b):
    return jnp.dot(a, b, precision=HIGH, preferred_element_type=F32)


def mm_t(a, b):
    return lax.dot_general(
        a, b, (((1,), (1,)), ((), ())), precision=HIGH, preferred_element_type=F32
    )


def t_mm(a, b):
    return lax.dot_general(
        a, b, (((0,), (0,)), ((), ())), precision=HIGH, preferred_element_type=F32
    )


def call(fn, outs, *args, scratch=()):
    vmem = pl.BlockSpec(memory_space=pltpu.VMEM)
    return pl.pallas_call(
        fn,
        out_shape=tuple(jax.ShapeDtypeStruct(shape, dtype) for shape, dtype in outs),
        in_specs=[pl.BlockSpec(memory_space=pltpu.VMEM)] * len(args),
        out_specs=tuple(vmem for _ in outs),
        scratch_shapes=list(scratch),
        compiler_params=pltpu.CompilerParams(vmem_limit_bytes=16 * 1024 * 1024),
    )(*args)


def block_pivots(a, n, below):
    row_id = lax.broadcasted_iota(jnp.int32, (n, 1), 0)
    for k in range(0, n, 2):
        row0, row1 = a[k : k + 1, :], a[k + 1 : k + 2, :]
        col0, col1 = a[:, k : k + 1], a[:, k + 1 : k + 2]
        p, q, r = row0[:, k : k + 1], row0[:, k + 1 : k + 2], row1[:, k + 1 : k + 2]
        inv = 1.0 / p
        ratio = q * inv
        inv_s = 1.0 / (r - q * ratio)
        row1 = row1 - ratio * row0
        col1 = col1 - ratio * col0
        if below:
            root0, root1 = lax.rsqrt(p), lax.rsqrt(r - q * ratio)
            new = a - jnp.where(row_id > k + 1, col0 * inv, 0.0) * row0
            new = new - jnp.where(row_id > k + 1, col1 * inv_s, 0.0) * row1
            a = jnp.where(row_id == k, row0 * root0, jnp.where(row_id == k + 1, row1 * root1, new))
        else:
            last = row1 * inv_s
            first = row0 * inv - ratio * last
            new = a - col0 * inv * row0 - col1 * last
            a = jnp.where(row_id == k, first, jnp.where(row_id == k + 1, last, new))
    return a[:, n:]


def forward(gram, right):
    return block_pivots(jnp.concatenate([gram, right], 1), gram.shape[0], True)


def identity(n):
    return (
        lax.broadcasted_iota(jnp.int32, (n, n), 0) == lax.broadcasted_iota(jnp.int32, (n, n), 1)
    ).astype(F32)


def solve(gram, right):
    return block_pivots(jnp.concatenate([gram, right], 1), gram.shape[0], False)


def spread_out(ref, chunk):
    for i in range(ref.shape[0]):
        ref[i] = chunk


def tree_sum(ref):
    parts = [ref[i] for i in range(ref.shape[0])]
    while len(parts) > 1:
        parts = [parts[i] + parts[i + 1] for i in range(0, len(parts), 2)]
    return parts[0]


def halves(ref, rows, side):
    lanes = slice(64 * side, 64 * side + 64)
    return jnp.concatenate([ref[i, rows, lanes] for i in range(ref.shape[0])], 1)


def split3(x):
    first = x.astype(BF16).astype(F32)
    second = (x - first).astype(BF16).astype(F32)
    return first, second, (x - first - second).astype(BF16).astype(F32)


def features(lefts, rights):
    out = [[], []]
    for left, right in zip(lefts, rights):
        for i, a in enumerate(left):
            for j, b in enumerate(right):
                if i + j < 3:
                    out[0].append(a)
                    out[1].append(b)
    n = len(out[0])
    for side in out:
        side.extend([jnp.zeros_like(side[0])] * (32 - n))
    return [jnp.concatenate(side, 0) for side in out]


def relay_kernel(block, twin, out):
    for i in range(out.shape[0]):
        out[i, 0:16] = block[...]
        out[i, 16:32] = twin[...]


def is_odd():
    return lax.rem(lax.axis_index("col"), 2) == 1


def swap_kernel(recv, out):
    odd = is_odd()
    for i in range(out.shape[0]):
        out[i, 0:8] = jnp.where(odd, recv[i, 0:8], recv[i, 16:24])
        out[i, 8:16] = jnp.where(odd, recv[i, 16:24], recv[i, 24:32])


def first_kernel(scale, delta2, recv, got, out, tile, power_near, left, right, split):
    odd = is_odd()
    count = recv.shape[0]
    near = [jnp.where(odd, got[i], recv[i, 0:16]) for i in range(count)]
    p = jnp.concatenate([x[:, :64] for x in near], 1)
    src = jnp.concatenate([x[0:8, 64:] for x in near], 1)
    far = []
    for i in range(count):
        far.append(jnp.where(odd, recv[i, 16:24], got[i, 8:16])[:, 64:])
        far.append(jnp.where(odd, recv[i, 0:8], got[i, 0:8])[:, 64:])
    t = jnp.concatenate(far, 1)[0:3] - 0.5
    power_near[...] = p
    high = p.astype(BF16)
    split[0:16] = high
    split[16:32] = (p - high.astype(F32)).astype(BF16)
    mean = jnp.broadcast_to(jnp.sum(src[4:5, :], 1, keepdims=True), (16, 16))
    extra = jnp.concatenate([mm_t(p, p), mean, jnp.zeros((16, 32), F32)], 1)
    s = src[0:3, :] - 0.5
    inv = 1.0 / (src[3:4, :] * scale)
    weight = inv * inv
    square = jnp.sum(s * s, 0, keepdims=True) + delta2
    one = jnp.ones((1, t.shape[1]), F32)
    lefts = [split3(-2.0 * s[k : k + 1] * weight) for k in range(3)]
    rights = [split3(t[k : k + 1]) for k in range(3)]
    lefts += [split3(square * weight), split3(weight)]
    rights += [(one,), split3(jnp.sum(t * t, 0, keepdims=True))]
    rows_l, rows_r = features(lefts, rights)
    left[...] = rows_l.T.astype(BF16)
    right[...] = rows_r.astype(BF16)

    @pl.loop(0, right.shape[1] // 256)
    def _(step):
        lanes = pl.ds(pl.multiple_of(step * 256, 256), 256)
        dist2 = jnp.dot(left[...], right[:, lanes], preferred_element_type=F32)
        block = lax.rsqrt(dist2).astype(BF16)
        tile[:, lanes] = block
        both = jnp.dot(split[...], block, preferred_element_type=F32)
        sums = both[:16] + both[16:]
        for i in range(4):
            out[step * 4 + i, :, :64] = sums[:, i * 64 : i * 64 + 64]
            out[step * 4 + i, :, 64:] = extra


def second_kernel(
    panels, recv, block, power_near, out, v_near, v_own, w_own, u_own, theta, factor, tmp
):
    total = tree_sum(recv)
    gram = total[:, 64:80]
    mean = total[0:1, 80:96] * (1.0 / panels)
    inverse = forward(gram, identity(gram.shape[0]))
    w = block[4:5, 64:] * block[:, :64] + total[:, :64]
    own = mm(inverse, jnp.concatenate([block[:, :64], w], 1))
    v, w = own[:, :64], own[:, 64:]
    u = w - mean[0:1, 0:1] * v
    tmp[:, :64] = u[:8]
    tmp[:, 64:] = u[8:]
    spread_out(out, tmp[...])
    theta[...] = mean
    factor[...] = mm(inverse, gram)
    v_near[...] = mm(inverse, power_near[...])
    v_own[...] = v
    w_own[...] = w
    u_own[...] = u


def third_kernel(recv, v_near, tile, out, u_split):
    u = jnp.concatenate([halves(recv, slice(0, 8), 0), halves(recv, slice(0, 8), 1)], 0)
    high = u.astype(BF16)
    u_split[0:16] = high
    u_split[16:32] = (u - high.astype(F32)).astype(BF16)
    extra = jnp.concatenate(
        [mm_t(v_near[...], u), mm_t(u, u), jnp.zeros((16, 32), F32)], 1
    )

    @pl.loop(0, tile.shape[1] // 256)
    def _(step):
        lanes = pl.ds(pl.multiple_of(step * 256, 256), 256)
        both = jnp.dot(u_split[...], tile[:, lanes], preferred_element_type=F32)
        sums = both[:16] + both[16:]
        for i in range(4):
            out[step * 4 + i, :, :64] = sums[:, i * 64 : i * 64 + 64]
            out[step * 4 + i, :, 64:] = extra


def fifth_kernel(
    recv, block, v_own, w_own, u_own, theta, factor, out, known, basis, images, tmp
):
    sums = tree_sum(recv)
    shifted = sums[:, 64:80]
    gram = sums[:, 80:96]
    v, w, u = v_own[...], w_own[...], u_own[...]
    x = block[4:5, 64:] * u + sums[:, :64]
    both = jnp.concatenate([x, u], 1) - t_mm(shifted, jnp.concatenate([w, v], 1))
    both = forward(gram - t_mm(shifted, shifted), both)
    small = mm_t(jnp.concatenate([w, both[:, :64], v], 0), both[:, :64])
    tmp[...] = jnp.zeros_like(tmp)
    for i in range(6):
        tmp[:, i * 16 : i * 16 + 16] = small[i * 8 : i * 8 + 8]
    spread_out(out, tmp[...])
    images[0:16] = w
    images[16:32] = both[:, :64]
    basis[0:16] = v
    basis[16:32] = both[:, 64:]
    shift = theta[0:1, 0:16] * identity(16)
    known[:, 0:16] = gram + theta[0:1, 0:16] * (shifted + shifted.T + shift)
    known[:, 16:32] = shifted.T + shift
    known[:, 32:48] = factor[...]


def sixth_kernel(recv, out):
    spread_out(out, tree_sum(recv))


def last_kernel(recv, known, basis, images, block, sol, res):
    total = tree_sum(recv)
    n12, n22, q2 = (
        jnp.concatenate([total[:, i : i + 16], total[:, i + 16 : i + 32]], 0)
        for i in (0, 32, 64)
    )
    system = jnp.concatenate(
        [
            jnp.concatenate([known[:, 0:16], n12, known[:, 16:32]], 1),
            jnp.concatenate([n12.T, n22, q2.T], 1),
        ],
        0,
    )
    coeff = mm(solve(system[:, :32], system[:, 32:]), known[:, 32:48])
    sol[...] = t_mm(coeff, basis[...])
    res[...] = block[:, :64] - t_mm(coeff, images[...])


def exchange(parts, axis, groups=None):
    return lax.all_to_all(parts, axis, 0, 0, axis_index_groups=groups)


def body(centroids, areas, conductance, power):
    nrhs, width = power.shape
    rows, cols = lax.axis_size("row"), lax.axis_size("col")
    panels = width * rows * cols
    scale = 4.0 / (math.pi * panels)
    delta2 = 16.0 / panels
    n_near, n_far = width * rows, width * cols
    own, square = ((nrhs, width), F32), ((nrhs, nrhs), F32)
    stack, fold = ((2 * nrhs, width), F32), [pltpu.VMEM((8, 128), F32)]
    twins = [(i, i ^ 1) for i in range(cols)]
    groups = [[r * cols + c for r in range(rows)] for c in range(0, cols, 2)]
    groups += [[r * cols + c for c in range(1, cols, 2)] for r in range(rows)]

    def place(x, row, lane):
        return jnp.pad(x, ((row, nrhs - row - x.shape[0]), (lane, 128 - lane - width)))

    block = (
        place(power, 0, 0)
        + place(centroids, 0, width)
        + place(areas[None, :], 3, width)
        + place(conductance[None, :], 4, width)
    )
    twin = lax.ppermute(block, "col", twins)
    (chunk,) = call(relay_kernel, [((rows, 2 * nrhs, 128), F32)], block, twin)
    recv = exchange(chunk, ("row", "col"), groups)
    (other,) = call(swap_kernel, [((rows, nrhs, 128), F32)], recv)
    got = lax.ppermute(other, "col", twins)
    parts, tile, power_near = call(
        functools.partial(first_kernel, scale, delta2),
        [((cols, 16, 128), F32), ((n_near, n_far), BF16), ((nrhs, n_near), F32)],
        recv, got,
        scratch=[
            pltpu.VMEM((n_near, 32), BF16),
            pltpu.VMEM((32, n_far), BF16),
            pltpu.VMEM((2 * nrhs, n_near), BF16),
        ],
    )
    recv = exchange(parts, "col")
    chunk, v_near, v_own, w_own, u_own, theta, factor = call(
        functools.partial(second_kernel, panels),
        [((rows, 8, 128), F32), ((nrhs, n_near), F32), own, own, own, ((1, nrhs), F32), square],
        recv, block, power_near,
        scratch=fold,
    )
    recv = exchange(chunk, "row")
    (parts,) = call(
        third_kernel, [((cols, 16, 128), F32)], recv, v_near, tile,
        scratch=[pltpu.VMEM((2 * nrhs, n_near), BF16)],
    )
    recv = exchange(parts, "col")
    chunk, known, basis, images = call(
        fifth_kernel, [((cols, 8, 128), F32), ((nrhs, 48), F32), stack, stack],
        recv, block, v_own, w_own, u_own, theta, factor,
        scratch=fold,
    )
    recv = exchange(chunk, "col")
    (chunk,) = call(sixth_kernel, [((rows, 8, 128), F32)], recv)
    recv = exchange(chunk, "row")
    return call(last_kernel, [own, own], recv, known, basis, images, block)


def solution(mesh):
    return jax.shard_map(
        body,
        mesh=mesh,
        in_specs=(
            P(None, ("col", "row")),
            P(("col", "row")),
            P(("col", "row")),
            P(None, ("col", "row")),
        ),
        out_specs=(P(None, ("col", "row")), P(None, ("col", "row"))),
        check_vma=False,
    )
```

time: 147 us -> 127 us (0.86)
  blocking collectives: 51.1 us -> 83.3 us
  waiting for transfers between devices: 29.7 us -> 1.77 us
  other arithmetic: 17.4 us -> 0.82 us
  Pallas kernels: 0 us -> 15.4 us
  matrix products: 9.74 us -> 0 us
  local copies, waits for them, and re-layouts: 6.63 us -> 0 us
  starting transfers between devices: 28.8 us -> 24.4 us
    all_to_all x4 -> x6, blocking collectives: 51.1 us -> 83.3 us  [exchange(): return lax.all_to_all(parts, axis, 0, 0, axis_index_groups=groups)]
    all_to_all x3 -> x0, waiting for transfers between devices: 29.7 us -> none  [spread(): lax.all_to_all(jnp.broadcast_to(chunk[None], (size,) + chunk.shape), axis...]
    all_to_all x3 -> x0, starting transfers between devices: 28.8 us -> none  [spread(): lax.all_to_all(jnp.broadcast_to(chunk[None], (size,) + chunk.shape), axis...]
    ppermute x0 -> x2, starting transfers between devices: none -> 24.4 us  [the longest x1 15.6 us: body(): got = lax.ppermute(other, 'col', twins)]
    pallas_call x0 -> x8, Pallas kernels: none -> 15.4 us  [call(): pl.pallas_call(fn, out_shape=tuple((jax.ShapeDtypeStruct(shape, dtype) fo...]
    another operation x10 -> x0, other arithmetic: 10.7 us -> none  [the longest x6 5.73 us: lower_inverse(): factor = jnp.linalg.cholesky(gram)]
    dot_general x10 -> x0, matrix products: 9.33 us -> none  [the longest x1 3.42 us: body(): jnp.dot(jnp.concatenate([high, low], 0), tile, preferred_element_type=jnp...]
    all_to_all x4 -> x0, other arithmetic: 3.55 us -> none  [the longest x2 1.9 us: scatter(): return jnp.sum(lax.all_to_all(parts, 'col', 0, 0), 0)]
  transfers between devices with their start and end apart: 3 -> 2, of which waited for: 3 -> 2; matrix products, arithmetic and copies ran while one was open for 1% -> 0% of each run, Pallas kernels for 0% -> 0%
where the time goes in v3:
time: 127 us; the launch traced here: 126 us
  blocking collectives  83.3 us (66%)
  starting transfers between devices  24.4 us (19%)
  Pallas kernels  15.4 us (12%)
  waiting for transfers between devices  1.77 us (1%)
    all_to_all x6, blocking collectives, exchange(): return lax.all_to_all(parts, axis, 0, 0, axis_index_groups=groups)  83.3 us
    ppermute x1, starting transfers between devices, body(): got = lax.ppermute(other, 'col', twins)  15.6 us
    pallas_call x8, Pallas kernels, call(): pl.pallas_call(fn, out_shape=tuple((jax.ShapeDtypeStruct(shape, dtype) fo...  15.4 us
    ppermute x1, starting transfers between devices, body(): twin = lax.ppermute(block, 'col', twins)  8.78 us
  transfers between devices with their start and end apart: 2, of which 2 were waited for; matrix products, arithmetic and copies ran while one was open for 0% of the time, Pallas kernels for 0%

profile of v3, /device:TPU:1, one launch (start us, length us, event | category | flops | bytes accessed | tf_op | source)
XLA Modules:
  0.0 126.3 jit_solution(12670080995579289028)
XLA Ops:
  0.6 0.8 pad_add_fusion.block
  1.5 8.8 %collective-permute-start = (f32[16,128]{1,0:T(8,128)S(1)}, f32[16,128]{1,0:T(8,128)S(1)}, u32[]{:S(2)}, u32[]{:S(2)}) collective-permute-start(f32[16,128]{1,0:T(8,128)S(1)} %pad_add_fusion.block), channel_id=1, source_target_pairs={{0,1},{1,0},{2,3},{3,2},{4,5},{5,4},{6,7},{7,6},{8,9},{9,8},{10,11... | collective-permute-start | bytes 24584 | tf_op jit(solution)/shard_map/ppermute | solution.py:293
  10.2 0.8 collective-permute-done.twin
  11.1 10.1 %all_to_all.30.recv = f32[16,32,128]{2,1,0:T(8,128)S(1)} all-to-all(f32[16,32,128]{2,1,0:T(8,128)S(1)} %shard_map.59), channel_id=1, replica_groups={{0,32,64,96,128,160,192,224,256,288,320,352,384,416,448,480},{2,34,66,9..., dimensions={0} | all-to-all | bytes 524288 | tf_op jit(solution)/shard_map/all_to_all | solution.py:268
  21.2 15.6 %collective-permute-start.1 = (f32[16,16,128]{2,1,0:T(8,128)S(1)}, f32[16,16,128]{2,1,0:T(8,128)S(1)}, u32[]{:S(2)}, u32[]{:S(2)}) collective-permute-start(f32[16,16,128]{2,1,0:T(8,128)S(1)} %shard_map.60), channel_id=1, source_target_pairs={{0,1},{1,0},{2,3},{3,2},{4,5},{5,4},{6,7},{7,6},{8,9},{9,8},{10,11... | collective-permute-start | bytes 393224 | tf_op jit(solution)/shard_map/ppermute | solution.py:297
  36.8 1.0 collective-permute-done.1.got
  37.8 5.1 %shard_map.61 = (f32[32,16,128]{2,1,0:T(8,128)S(1)}, bf16[1024,2048]{1,0:T(8,128)(2,1)S(1)}, f32[16,1024]{1,0:T(8,128)S(1)}) custom-call(f32[16,32,128]{2,1,0:T(8,128)S(1)} %all_to_all.30.recv, f32[16,16,128]{2,1,0:T(8,128)S(1)} %collective-permute-done.1.got), custom_call_target="tpu_custom_call" | custom-call | tf_op jit(solution)/shard_map/pallas_call | solution.py:34
  42.8 16.1 %all_to_all.31.recv = f32[32,16,128]{2,1,0:T(8,128)S(1)} all-to-all(f32[32,16,128]{2,1,0:T(8,128)S(1)} %get-tuple-element.16), channel_id=1, replica_groups=mesh['row'=16,'col'=32] {'col'}, dimensions={0} | all-to-all | bytes 524288 | tf_op jit(solution)/shard_map/all_to_all | solution.py:268
  58.9 1.7 %shard_map.62 = (f32[16,8,128]{2,1,0:T(8,128)S(1)}, f32[16,1024]{1,0:T(8,128)S(1)}, f32[16,64]{1,0:T(8,128)S(1)}, f32[16,64]{1,0:T(8,128)S(1)}, f32[16,64]{1,0:T...) custom-call(f32[32,16,128]{2,1,0:T(8,128)S(1)} %all_to_all.31.recv, f32[16,128]{1,0:T(8,128)S(1)} %pad_add_fusion.block, ...), custom_call_target="tpu_custom_call" | custom-call | tf_op jit(solution)/shard_map/pallas_call | solution.py:34
  60.7 17.3 %all_to_all.32.recv = f32[16,8,128]{2,1,0:T(8,128)S(1)} all-to-all(f32[16,8,128]{2,1,0:T(8,128)S(1)} %get-tuple-element.18), channel_id=1, replica_groups=mesh['row'=16,'col'=32] {'row'}, dimensions={0} | all-to-all | bytes 131072 | tf_op jit(solution)/shard_map/all_to_all | solution.py:268
  78.0 2.6 %shard_map.63 = f32[32,16,128]{2,1,0:T(8,128)S(1)} custom-call(f32[16,8,128]{2,1,0:T(8,128)S(1)} %all_to_all.32.recv, f32[16,1024]{1,0:T(8,128)S(1)} %get-tuple-element.19.v_near, bf16[1024,2048]{1,0:T(8,128)(2,1)S(1)} %get-tuple-element.20.tile), custom_call_target="tpu_custom_call" | custom-call | tf_op jit(solution)/shard_map/pallas_call | solution.py:34
  80.6 14.3 %all_to_all.33.recv = f32[32,16,128]{2,1,0:T(8,128)S(1)} all-to-all(f32[32,16,128]{2,1,0:T(8,128)S(1)} %shard_map.63), channel_id=1, replica_groups=mesh['row'=16,'col'=32] {'col'}, dimensions={0} | all-to-all | bytes 524288 | tf_op jit(solution)/shard_map/all_to_all | solution.py:268
  94.9 2.0 %shard_map.64 = (f32[32,8,128]{2,1,0:T(8,128)S(1)}, f32[16,48]{1,0:T(8,128)S(1)}, f32[32,64]{1,0:T(8,128)S(1)}, f32[32,64]{1,0:T(8,128)S(1)}) custom-call(f32[32,16,128]{2,1,0:T(8,128)S(1)} %all_to_all.33.recv, f32[16,128]{1,0:T(8,128)S(1)} %pad_add_fusion.block, f32[16,64]{1,0:T(8,128)S(1)} %get-tuple-element.21.v_own, ...), custom_call_target="tpu_custom_call" | custom-call | tf_op jit(solution)/shard_map/pallas_call | solution.py:34
  96.9 11.2 %all_to_all.34.recv = f32[32,8,128]{2,1,0:T(8,128)S(1)} all-to-all(f32[32,8,128]{2,1,0:T(8,128)S(1)} %get-tuple-element.26), channel_id=1, replica_groups=mesh['row'=16,'col'=32] {'col'}, dimensions={0} | all-to-all | bytes 262144 | tf_op jit(solution)/shard_map/all_to_all | solution.py:268
  108.1 14.3 %all_to_all.35.recv = f32[16,8,128]{2,1,0:T(8,128)S(1)} all-to-all(f32[16,8,128]{2,1,0:T(8,128)S(1)} %shard_map.65), channel_id=1, replica_groups=mesh['row'=16,'col'=32] {'row'}, dimensions={0} | all-to-all | bytes 131072 | tf_op jit(solution)/shard_map/all_to_all | solution.py:268
  122.4 3.9 %shard_map.66 = (f32[16,64]{1,0:T(8,128)}, f32[16,64]{1,0:T(8,128)}) custom-call(f32[16,8,128]{2,1,0:T(8,128)S(1)} %all_to_all.35.recv, f32[16,48]{1,0:T(8,128)S(1)} %get-tuple-element.27.known, f32[32,64]{1,0:T(8,128)S(1)} %get-tuple-element.28.basis, f32[32,64]{1,0:T(8,128)S(1)} %get-tuple-element.29.images, f32[16,128]{1,0:T(8,128)S(1)} %pad_add_fusion.block), custom_call_target="tpu_custom_call" | custom-call | tf_op jit(solution)/shard_map/pallas_call | solution.py:34
  (3 shorter events, 0.1 us)
Async XLA Ops:
  1.5 9.6 %collective-permute-start = (f32[16,128]{1,0:T(8,128)S(1)}, f32[16,128]{1,0:T(8,128)S(1)}, u32[]{:S(2)}, u32[]{:S(2)}) collective-permute-start(f32[16,128]{1,0:T(8,128)S(1)} %pad_add_fusion.block), channel_id=1, source_target_pairs={{0,1},{1,0},{2,3},{3,2},{4,5},{5,4},{6,7},{7,6},{8,9},{9,8},{10,11... | collective-permute-start | bytes 24584 | tf_op jit(solution)/shard_map/ppermute | solution.py:293
  21.2 16.5 %collective-permute-start.1 = (f32[16,16,128]{2,1,0:T(8,128)S(1)}, f32[16,16,128]{2,1,0:T(8,128)S(1)}, u32[]{:S(2)}, u32[]{:S(2)}) collective-permute-start(f32[16,16,128]{2,1,0:T(8,128)S(1)} %shard_map.60), channel_id=1, source_target_pairs={{0,1},{1,0},{2,3},{3,2},{4,5},{5,4},{6,7},{7,6},{8,9},{9,8},{10,11... | collective-permute-start | bytes 393224 | tf_op jit(solution)/shard_map/ppermute | solution.py:297

commit v4 on v3

--- a/solution.py
+++ b/solution.py
@@ -47,21 +47,15 @@
         row0, row1 = a[k : k + 1, :], a[k + 1 : k + 2, :]
         col0, col1 = a[:, k : k + 1], a[:, k + 1 : k + 2]
         p, q, r = row0[:, k : k + 1], row0[:, k + 1 : k + 2], row1[:, k + 1 : k + 2]
-        inv = 1.0 / p
-        ratio = q * inv
-        inv_s = 1.0 / (r - q * ratio)
-        row1 = row1 - ratio * row0
-        col1 = col1 - ratio * col0
+        det = p * r - q * q
+        inv = 1.0 / det
+        mix0, mix1 = r * row0 - q * row1, p * row1 - q * row0
+        first, last = mix0 * inv, mix1 * inv
+        new = a - col0 * first - col1 * last
         if below:
-            root0, root1 = lax.rsqrt(p), lax.rsqrt(r - q * ratio)
-            new = a - jnp.where(row_id > k + 1, col0 * inv, 0.0) * row0
-            new = new - jnp.where(row_id > k + 1, col1 * inv_s, 0.0) * row1
-            a = jnp.where(row_id == k, row0 * root0, jnp.where(row_id == k + 1, row1 * root1, new))
-        else:
-            last = row1 * inv_s
-            first = row0 * inv - ratio * last
-            new = a - col0 * inv * row0 - col1 * last
-            a = jnp.where(row_id == k, first, jnp.where(row_id == k + 1, last, new))
+            first, last = row0 * lax.rsqrt(p), mix1 * lax.rsqrt(p * det)
+            new = jnp.where(row_id > k, new, a)
+        a = jnp.where(row_id == k, first, jnp.where(row_id == k + 1, last, new))
     return a[:, n:]
 
 
@@ -117,9 +111,7 @@
 
 
 def relay_kernel(block, twin, out):
-    for i in range(out.shape[0]):
-        out[i, 0:16] = block[...]
-        out[i, 16:32] = twin[...]
+    spread_out(out, jnp.concatenate([block[...], twin[...]], 1))
 
 
 def is_odd():
@@ -129,27 +121,27 @@
 def swap_kernel(recv, out):
     odd = is_odd()
     for i in range(out.shape[0]):
-        out[i, 0:8] = jnp.where(odd, recv[i, 0:8], recv[i, 16:24])
-        out[i, 8:16] = jnp.where(odd, recv[i, 16:24], recv[i, 24:32])
+        places = recv[i, 16:24]
+        out[i, 0:8, :64] = jnp.where(odd, places[:, :64], recv[i, 0:8, 64:])
+        out[i, 0:8, 64:] = places[:, 64:]
+        out[i, 8:16, :64] = recv[i, 8:16, 64:]
+        out[i, 8:16, 64:] = places[:, 64:]
 
 
 def first_kernel(scale, delta2, recv, got, out, tile, power_near, left, right, split):
     odd = is_odd()
     count = recv.shape[0]
-    near = [jnp.where(odd, got[i], recv[i, 0:16]) for i in range(count)]
-    p = jnp.concatenate([x[:, :64] for x in near], 1)
-    src = jnp.concatenate([x[0:8, 64:] for x in near], 1)
+    p = jnp.concatenate(
+        [jnp.where(odd, got[i, :, :64], recv[i, 0:16, :64]) for i in range(count)], 1
+    )
+    src = jnp.concatenate(
+        [jnp.where(odd, got[i, 0:8, 64:], recv[i, 16:24, :64]) for i in range(count)], 1
+    )
     far = []
     for i in range(count):
-        far.append(jnp.where(odd, recv[i, 16:24], got[i, 8:16])[:, 64:])
-        far.append(jnp.where(odd, recv[i, 0:8], got[i, 0:8])[:, 64:])
+        far.append(jnp.where(odd, recv[i, 16:24, 64:], got[i, 0:8, 64:]))
+        far.append(jnp.where(odd, recv[i, 16:24, :64], got[i, 0:8, :64]))
     t = jnp.concatenate(far, 1)[0:3] - 0.5
-    power_near[...] = p
-    high = p.astype(BF16)
-    split[0:16] = high
-    split[16:32] = (p - high.astype(F32)).astype(BF16)
-    mean = jnp.broadcast_to(jnp.sum(src[4:5, :], 1, keepdims=True), (16, 16))
-    extra = jnp.concatenate([mm_t(p, p), mean, jnp.zeros((16, 32), F32)], 1)
     s = src[0:3, :] - 0.5
     inv = 1.0 / (src[3:4, :] * scale)
     weight = inv * inv
@@ -162,18 +154,25 @@
     rows_l, rows_r = features(lefts, rights)
     left[...] = rows_l.T.astype(BF16)
     right[...] = rows_r.astype(BF16)
-
-    @pl.loop(0, right.shape[1] // 256)
-    def _(step):
-        lanes = pl.ds(pl.multiple_of(step * 256, 256), 256)
+    power_near[...] = p
+    high = p.astype(BF16)
+    split[0:16] = high
+    split[16:32] = (p - high.astype(F32)).astype(BF16)
+    mean = jnp.broadcast_to(jnp.sum(src[4:5, :], 1, keepdims=True), (16, 16))
+    extra = jnp.concatenate([mm_t(p, p), mean, jnp.zeros((16, 32), F32)], 1)
+    for step in range(right.shape[1] // 256):
+        lanes = slice(step * 256, step * 256 + 256)
         dist2 = jnp.dot(left[...], right[:, lanes], preferred_element_type=F32)
-        block = lax.rsqrt(dist2).astype(BF16)
-        tile[:, lanes] = block
-        both = jnp.dot(split[...], block, preferred_element_type=F32)
-        sums = both[:16] + both[16:]
-        for i in range(4):
-            out[step * 4 + i, :, :64] = sums[:, i * 64 : i * 64 + 64]
-            out[step * 4 + i, :, 64:] = extra
+        tile[:, lanes] = lax.rsqrt(dist2).astype(BF16)
+    image(split, tile, extra, out)
+
+
+def image(split, tile, extra, out):
+    both = jnp.dot(split[...], tile[...], preferred_element_type=F32)
+    sums = both[:16] + both[16:]
+    for i in range(out.shape[0]):
+        out[i, :, :64] = sums[:, i * 64 : i * 64 + 64]
+        out[i, :, 64:] = extra
 
 
 def second_kernel(
@@ -183,8 +182,8 @@
     gram = total[:, 64:80]
     mean = total[0:1, 80:96] * (1.0 / panels)
     inverse = forward(gram, identity(gram.shape[0]))
-    w = block[4:5, 64:] * block[:, :64] + total[:, :64]
-    own = mm(inverse, jnp.concatenate([block[:, :64], w], 1))
+    w = block[20:21, :] * block[0:16, :] + total[:, :64]
+    own = mm(inverse, jnp.concatenate([block[0:16, :], w], 1))
     v, w = own[:, :64], own[:, 64:]
     u = w - mean[0:1, 0:1] * v
     tmp[:, :64] = u[:8]
@@ -206,15 +205,7 @@
     extra = jnp.concatenate(
         [mm_t(v_near[...], u), mm_t(u, u), jnp.zeros((16, 32), F32)], 1
     )
-
-    @pl.loop(0, tile.shape[1] // 256)
-    def _(step):
-        lanes = pl.ds(pl.multiple_of(step * 256, 256), 256)
-        both = jnp.dot(u_split[...], tile[:, lanes], preferred_element_type=F32)
-        sums = both[:16] + both[16:]
-        for i in range(4):
-            out[step * 4 + i, :, :64] = sums[:, i * 64 : i * 64 + 64]
-            out[step * 4 + i, :, 64:] = extra
+    image(u_split, tile, extra, out)
 
 
 def fifth_kernel(
@@ -224,7 +215,7 @@
     shifted = sums[:, 64:80]
     gram = sums[:, 80:96]
     v, w, u = v_own[...], w_own[...], u_own[...]
-    x = block[4:5, 64:] * u + sums[:, :64]
+    x = block[20:21, :] * u + sums[:, :64]
     both = jnp.concatenate([x, u], 1) - t_mm(shifted, jnp.concatenate([w, v], 1))
     both = forward(gram - t_mm(shifted, shifted), both)
     small = mm_t(jnp.concatenate([w, both[:, :64], v], 0), both[:, :64])
@@ -261,7 +252,7 @@
     )
     coeff = mm(solve(system[:, :32], system[:, 32:]), known[:, 32:48])
     sol[...] = t_mm(coeff, basis[...])
-    res[...] = block[:, :64] - t_mm(coeff, images[...])
+    res[...] = block[0:16, :] - t_mm(coeff, images[...])
 
 
 def exchange(parts, axis, groups=None):
@@ -281,17 +272,17 @@
     groups = [[r * cols + c for r in range(rows)] for c in range(0, cols, 2)]
     groups += [[r * cols + c for c in range(1, cols, 2)] for r in range(rows)]
 
-    def place(x, row, lane):
-        return jnp.pad(x, ((row, nrhs - row - x.shape[0]), (lane, 128 - lane - width)))
+    def place(x, row):
+        return jnp.pad(x, ((row, nrhs + 8 - row - x.shape[0]), (0, 0)))
 
     block = (
-        place(power, 0, 0)
-        + place(centroids, 0, width)
-        + place(areas[None, :], 3, width)
-        + place(conductance[None, :], 4, width)
+        place(power, 0)
+        + place(centroids, nrhs)
+        + place(areas[None, :], nrhs + 3)
+        + place(conductance[None, :], nrhs + 4)
     )
     twin = lax.ppermute(block, "col", twins)
-    (chunk,) = call(relay_kernel, [((rows, 2 * nrhs, 128), F32)], block, twin)
+    (chunk,) = call(relay_kernel, [((rows, nrhs + 8, 128), F32)], block, twin)
     recv = exchange(chunk, ("row", "col"), groups)
     (other,) = call(swap_kernel, [((rows, nrhs, 128), F32)], recv)
     got = lax.ppermute(other, "col", twins)

time: 127 us -> 121 us (0.953)
  Pallas kernels: 15.4 us -> 10.9 us
  blocking collectives: 83.3 us -> 81.9 us
    pallas_call x8, Pallas kernels: 15.4 us -> 10.9 us  [call(): pl.pallas_call(fn, out_shape=tuple((jax.ShapeDtypeStruct(shape, dtype) fo...]
    all_to_all x6, blocking collectives: 83.3 us -> 81.9 us  [exchange(): return lax.all_to_all(parts, axis, 0, 0, axis_index_groups=groups)]
where the time goes in v4:
time: 121 us; the launch traced here: 120 us
  blocking collectives  81.9 us (68%)
  starting transfers between devices  24.4 us (20%)
  Pallas kernels  10.9 us (9%)
  waiting for transfers between devices  1.78 us (1%)
    all_to_all x6, blocking collectives, exchange(): return lax.all_to_all(parts, axis, 0, 0, axis_index_groups=groups)  81.9 us
    ppermute x1, starting transfers between devices, body(): got = lax.ppermute(other, 'col', twins)  15.6 us
    pallas_call x8, Pallas kernels, call(): pl.pallas_call(fn, out_shape=tuple((jax.ShapeDtypeStruct(shape, dtype) fo...  10.9 us
    ppermute x1, starting transfers between devices, body(): twin = lax.ppermute(block, 'col', twins)  8.77 us
  transfers between devices with their start and end apart: 2, of which 2 were waited for; matrix products, arithmetic and copies ran while one was open for 0% of the time, Pallas kernels for 0%

profile of v4, /device:TPU:1, one launch (start us, length us, event | category | flops | bytes accessed | tf_op | source)
XLA Modules:
  0.0 120.4 jit_solution(17733035350076397432)
XLA Ops:
  0.6 0.8 pad_add_fusion.block
  1.4 8.8 %collective-permute-start = (f32[24,64]{1,0:T(8,128)S(1)}, f32[24,64]{1,0:T(8,128)S(1)}, u32[]{:S(2)}, u32[]{:S(2)}) collective-permute-start(f32[24,64]{1,0:T(8,128)S(1)} %pad_add_fusion.block), channel_id=1, source_target_pairs={{0,1},{1,0},{2,3},{3,2},{4,5},{5,4},{6,7},{7,6},{8,9},{9,8},{10,11... | collective-permute-start | bytes 18440 | tf_op jit(solution)/shard_map/ppermute | solution.py:284
  10.2 0.8 collective-permute-done.twin
  11.0 0.1 shard_map.59
  11.1 9.8 %all_to_all.30.recv = f32[16,24,128]{2,1,0:T(8,128)S(1)} all-to-all(f32[16,24,128]{2,1,0:T(8,128)S(1)} %shard_map.59), channel_id=1, replica_groups={{0,32,64,96,128,160,192,224,256,288,320,352,384,416,448,480},{2,34,66,9..., dimensions={0} | all-to-all | bytes 393216 | tf_op jit(solution)/shard_map/all_to_all | solution.py:259
  20.9 0.1 shard_map.60
  21.0 15.6 %collective-permute-start.1 = (f32[16,16,128]{2,1,0:T(8,128)S(1)}, f32[16,16,128]{2,1,0:T(8,128)S(1)}, u32[]{:S(2)}, u32[]{:S(2)}) collective-permute-start(f32[16,16,128]{2,1,0:T(8,128)S(1)} %shard_map.60), channel_id=1, source_target_pairs={{0,1},{1,0},{2,3},{3,2},{4,5},{5,4},{6,7},{7,6},{8,9},{9,8},{10,11... | collective-permute-start | bytes 393224 | tf_op jit(solution)/shard_map/ppermute | solution.py:288
  36.5 1.0 collective-permute-done.1.got
  37.5 2.3 %shard_map.61 = (f32[32,16,128]{2,1,0:T(8,128)S(1)}, bf16[1024,2048]{1,0:T(8,128)(2,1)S(1)}, f32[16,1024]{1,0:T(8,128)S(1)}) custom-call(f32[16,24,128]{2,1,0:T(8,128)S(1)} %all_to_all.30.recv, f32[16,16,128]{2,1,0:T(8,128)S(1)} %collective-permute-done.1.got), custom_call_target="tpu_custom_call" | custom-call | tf_op jit(solution)/shard_map/pallas_call | solution.py:34
  39.9 16.2 %all_to_all.31.recv = f32[32,16,128]{2,1,0:T(8,128)S(1)} all-to-all(f32[32,16,128]{2,1,0:T(8,128)S(1)} %get-tuple-element.16), channel_id=1, replica_groups=mesh['row'=16,'col'=32] {'col'}, dimensions={0} | all-to-all | bytes 524288 | tf_op jit(solution)/shard_map/all_to_all | solution.py:259
  56.0 1.7 %shard_map.62 = (f32[16,8,128]{2,1,0:T(8,128)S(1)}, f32[16,1024]{1,0:T(8,128)S(1)}, f32[16,64]{1,0:T(8,128)S(1)}, f32[16,64]{1,0:T(8,128)S(1)}, f32[16,64]{1,0:T...) custom-call(f32[32,16,128]{2,1,0:T(8,128)S(1)} %all_to_all.31.recv, f32[24,64]{1,0:T(8,128)S(1)} %pad_add_fusion.block, ...), custom_call_target="tpu_custom_call" | custom-call | tf_op jit(solution)/shard_map/pallas_call | solution.py:34
  57.7 16.2 %all_to_all.32.recv = f32[16,8,128]{2,1,0:T(8,128)S(1)} all-to-all(f32[16,8,128]{2,1,0:T(8,128)S(1)} %get-tuple-element.18), channel_id=1, replica_groups=mesh['row'=16,'col'=32] {'row'}, dimensions={0} | all-to-all | bytes 131072 | tf_op jit(solution)/shard_map/all_to_all | solution.py:259
  73.8 1.1 shard_map.63
  75.0 14.3 %all_to_all.33.recv = f32[32,16,128]{2,1,0:T(8,128)S(1)} all-to-all(f32[32,16,128]{2,1,0:T(8,128)S(1)} %shard_map.63), channel_id=1, replica_groups=mesh['row'=16,'col'=32] {'col'}, dimensions={0} | all-to-all | bytes 524288 | tf_op jit(solution)/shard_map/all_to_all | solution.py:259
  89.2 2.0 %shard_map.64 = (f32[32,8,128]{2,1,0:T(8,128)S(1)}, f32[16,48]{1,0:T(8,128)S(1)}, f32[32,64]{1,0:T(8,128)S(1)}, f32[32,64]{1,0:T(8,128)S(1)}) custom-call(f32[32,16,128]{2,1,0:T(8,128)S(1)} %all_to_all.33.recv, f32[24,64]{1,0:T(8,128)S(1)} %pad_add_fusion.block, f32[16,64]{1,0:T(8,128)S(1)} %get-tuple-element.21.v_own, ...), custom_call_target="tpu_custom_call" | custom-call | tf_op jit(solution)/shard_map/pallas_call | solution.py:34
  91.2 11.2 %all_to_all.34.recv = f32[32,8,128]{2,1,0:T(8,128)S(1)} all-to-all(f32[32,8,128]{2,1,0:T(8,128)S(1)} %get-tuple-element.26), channel_id=1, replica_groups=mesh['row'=16,'col'=32] {'col'}, dimensions={0} | all-to-all | bytes 262144 | tf_op jit(solution)/shard_map/all_to_all | solution.py:259
  102.4 14.3 %all_to_all.35.recv = f32[16,8,128]{2,1,0:T(8,128)S(1)} all-to-all(f32[16,8,128]{2,1,0:T(8,128)S(1)} %shard_map.65), channel_id=1, replica_groups=mesh['row'=16,'col'=32] {'row'}, dimensions={0} | all-to-all | bytes 131072 | tf_op jit(solution)/shard_map/all_to_all | solution.py:259
  116.7 3.7 %shard_map.66 = (f32[16,64]{1,0:T(8,128)}, f32[16,64]{1,0:T(8,128)}) custom-call(f32[16,8,128]{2,1,0:T(8,128)S(1)} %all_to_all.35.recv, f32[16,48]{1,0:T(8,128)S(1)} %get-tuple-element.27.known, f32[32,64]{1,0:T(8,128)S(1)} %get-tuple-element.28.basis, f32[32,64]{1,0:T(8,128)S(1)} %get-tuple-element.29.images, f32[24,64]{1,0:T(8,128)S(1)} %pad_add_fusion.block), custom_call_target="tpu_custom_call" | custom-call | tf_op jit(solution)/shard_map/pallas_call | solution.py:34
  (1 shorter events, 0.0 us)
Async XLA Ops:
  1.4 9.6 %collective-permute-start = (f32[24,64]{1,0:T(8,128)S(1)}, f32[24,64]{1,0:T(8,128)S(1)}, u32[]{:S(2)}, u32[]{:S(2)}) collective-permute-start(f32[24,64]{1,0:T(8,128)S(1)} %pad_add_fusion.block), channel_id=1, source_target_pairs={{0,1},{1,0},{2,3},{3,2},{4,5},{5,4},{6,7},{7,6},{8,9},{9,8},{10,11... | collective-permute-start | bytes 18440 | tf_op jit(solution)/shard_map/ppermute | solution.py:284
  21.0 16.6 %collective-permute-start.1 = (f32[16,16,128]{2,1,0:T(8,128)S(1)}, f32[16,16,128]{2,1,0:T(8,128)S(1)}, u32[]{:S(2)}, u32[]{:S(2)}) collective-permute-start(f32[16,16,128]{2,1,0:T(8,128)S(1)} %shard_map.60), channel_id=1, source_target_pairs={{0,1},{1,0},{2,3},{3,2},{4,5},{5,4},{6,7},{7,6},{8,9},{9,8},{10,11... | collective-permute-start | bytes 393224 | tf_op jit(solution)/shard_map/ppermute | solution.py:288

commit v5 on v4

--- a/solution.py
+++ b/solution.py
@@ -41,36 +41,39 @@
     )(*args)
 
 
-def block_pivots(a, n, below):
-    row_id = lax.broadcasted_iota(jnp.int32, (n, 1), 0)
-    for k in range(0, n, 2):
-        row0, row1 = a[k : k + 1, :], a[k + 1 : k + 2, :]
-        col0, col1 = a[:, k : k + 1], a[:, k + 1 : k + 2]
-        p, q, r = row0[:, k : k + 1], row0[:, k + 1 : k + 2], row1[:, k + 1 : k + 2]
-        det = p * r - q * q
-        inv = 1.0 / det
-        mix0, mix1 = r * row0 - q * row1, p * row1 - q * row0
-        first, last = mix0 * inv, mix1 * inv
-        new = a - col0 * first - col1 * last
-        if below:
-            first, last = row0 * lax.rsqrt(p), mix1 * lax.rsqrt(p * det)
-            new = jnp.where(row_id > k, new, a)
-        a = jnp.where(row_id == k, first, jnp.where(row_id == k + 1, last, new))
-    return a[:, n:]
-
-
-def forward(gram, right):
-    return block_pivots(jnp.concatenate([gram, right], 1), gram.shape[0], True)
+def eliminate(gram, right, below):
+    n = gram.shape[0]
+    width = n + right.shape[1]
+    count = -(-width // 128)
+    parts = [gram, right]
+    if count * 128 > width:
+        parts.append(jnp.zeros((n, count * 128 - width), F32))
+    a = jnp.concatenate(parts, 1)
+    tiles = [a[:, i * 128 : i * 128 + 128] for i in range(count)]
+
+    def full(x):
+        return jnp.broadcast_to(x, (n, 128))
+
+    row_id = lax.broadcasted_iota(jnp.int32, (n, 128), 0)
+    scale = jnp.zeros((n, 128), F32)
+    for start in range(0, n, 16):
+        cols = [full(tiles[0][:, start + i : start + i + 1]) for i in range(16)]
+        for i in range(16):
+            k = start + i
+            pivot = full(cols[i][k : k + 1, :])
+            inv = 1.0 / pivot
+            mask = row_id > k if below else row_id != k
+            scale = jnp.where(row_id == k, lax.rsqrt(pivot) if below else inv, scale)
+            factor = jnp.where(mask, cols[i], 0.0) * inv
+            tiles = [t - factor * full(t[k : k + 1, :]) for t in tiles]
+            cols = cols[: i + 1] + [c - factor * full(c[k : k + 1, :]) for c in cols[i + 1 :]]
+    return jnp.concatenate([t * scale for t in tiles], 1)[:, n:width]
 
 
 def identity(n):
     return (
         lax.broadcasted_iota(jnp.int32, (n, n), 0) == lax.broadcasted_iota(jnp.int32, (n, n), 1)
     ).astype(F32)
-
-
-def solve(gram, right):
-    return block_pivots(jnp.concatenate([gram, right], 1), gram.shape[0], False)
 
 
 def spread_out(ref, chunk):
@@ -181,19 +184,19 @@
     total = tree_sum(recv)
     gram = total[:, 64:80]
     mean = total[0:1, 80:96] * (1.0 / panels)
-    inverse = forward(gram, identity(gram.shape[0]))
-    w = block[20:21, :] * block[0:16, :] + total[:, :64]
-    own = mm(inverse, jnp.concatenate([block[0:16, :], w], 1))
-    v, w = own[:, :64], own[:, 64:]
-    u = w - mean[0:1, 0:1] * v
+    p = block[0:16, :]
+    u = (block[20:21, :] - mean[0:1, 0:1]) * p + total[:, :64]
+    both = eliminate(gram, jnp.concatenate([identity(16), u], 1), True)
+    inverse, u = both[:, :16], both[:, 16:]
     tmp[:, :64] = u[:8]
     tmp[:, 64:] = u[8:]
     spread_out(out, tmp[...])
+    v = mm(inverse, p)
     theta[...] = mean
     factor[...] = mm(inverse, gram)
     v_near[...] = mm(inverse, power_near[...])
     v_own[...] = v
-    w_own[...] = w
+    w_own[...] = u + mean[0:1, 0:1] * v
     u_own[...] = u
 
 
@@ -217,8 +220,8 @@
     v, w, u = v_own[...], w_own[...], u_own[...]
     x = block[20:21, :] * u + sums[:, :64]
     both = jnp.concatenate([x, u], 1) - t_mm(shifted, jnp.concatenate([w, v], 1))
-    both = forward(gram - t_mm(shifted, shifted), both)
-    small = mm_t(jnp.concatenate([w, both[:, :64], v], 0), both[:, :64])
+    both = eliminate(gram - t_mm(shifted, shifted), both, True)
+    small = mm_t(jnp.concatenate([w, both[:, :64], block[0:16, :]], 0), both[:, :64])
     tmp[...] = jnp.zeros_like(tmp)
     for i in range(6):
         tmp[:, i * 16 : i * 16 + 16] = small[i * 8 : i * 8 + 8]
@@ -229,8 +232,7 @@
     basis[16:32] = both[:, 64:]
     shift = theta[0:1, 0:16] * identity(16)
     known[:, 0:16] = gram + theta[0:1, 0:16] * (shifted + shifted.T + shift)
-    known[:, 16:32] = shifted.T + shift
-    known[:, 32:48] = factor[...]
+    known[:, 16:32] = mm(shifted.T + shift, factor[...])
 
 
 def sixth_kernel(recv, out):
@@ -250,7 +252,7 @@
         ],
         0,
     )
-    coeff = mm(solve(system[:, :32], system[:, 32:]), known[:, 32:48])
+    coeff = eliminate(system[:, :32], system[:, 32:], False)
     sol[...] = t_mm(coeff, basis[...])
     res[...] = block[0:16, :] - t_mm(coeff, images[...])
 
@@ -310,7 +312,7 @@
     )
     recv = exchange(parts, "col")
     chunk, known, basis, images = call(
-        fifth_kernel, [((cols, 8, 128), F32), ((nrhs, 48), F32), stack, stack],
+        fifth_kernel, [((cols, 8, 128), F32), ((nrhs, 2 * nrhs), F32), stack, stack],
         recv, block, v_own, w_own, u_own, theta, factor,
         scratch=fold,
     )

time: 121 us -> 117 us (0.967)
  Pallas kernels: 10.9 us -> 7.39 us
    pallas_call x8, Pallas kernels: 10.9 us -> 7.39 us  [call(): pl.pallas_call(fn, out_shape=tuple((jax.ShapeDtypeStruct(shape, dtype) fo...]
where the time goes in v5:
time: 117 us
  blocking collectives  81.9 us (70%)
  starting transfers between devices  24.4 us (21%)
  Pallas kernels  7.39 us (6%)
  waiting for transfers between devices  1.78 us (2%)
    all_to_all x6, blocking collectives, exchange(): return lax.all_to_all(parts, axis, 0, 0, axis_index_groups=groups)  81.9 us
    ppermute x1, starting transfers between devices, body(): got = lax.ppermute(other, 'col', twins)  15.6 us
    ppermute x1, starting transfers between devices, body(): twin = lax.ppermute(block, 'col', twins)  8.77 us
    pallas_call x8, Pallas kernels, call(): pl.pallas_call(fn, out_shape=tuple((jax.ShapeDtypeStruct(shape, dtype) fo...  7.39 us
  transfers between devices with their start and end apart: 2, of which 2 were waited for; matrix products, arithmetic and copies ran while one was open for 0% of the time, Pallas kernels for 0%

profile of v5, /device:TPU:1, one launch (start us, length us, event | category | flops | bytes accessed | tf_op | source)
XLA Modules:
  0.0 116.8 jit_solution(13158474210229232710)
XLA Ops:
  0.6 0.8 pad_add_fusion.block
  1.4 8.8 %collective-permute-start = (f32[24,64]{1,0:T(8,128)S(1)}, f32[24,64]{1,0:T(8,128)S(1)}, u32[]{:S(2)}, u32[]{:S(2)}) collective-permute-start(f32[24,64]{1,0:T(8,128)S(1)} %pad_add_fusion.block), channel_id=1, source_target_pairs={{0,1},{1,0},{2,3},{3,2},{4,5},{5,4},{6,7},{7,6},{8,9},{9,8},{10,11... | collective-permute-start | bytes 18440 | tf_op jit(solution)/shard_map/ppermute | solution.py:286
  10.2 0.8 collective-permute-done.twin
  11.0 0.1 shard_map.59
  11.1 9.8 %all_to_all.30.recv = f32[16,24,128]{2,1,0:T(8,128)S(1)} all-to-all(f32[16,24,128]{2,1,0:T(8,128)S(1)} %shard_map.59), channel_id=1, replica_groups={{0,32,64,96,128,160,192,224,256,288,320,352,384,416,448,480},{2,34,66,9..., dimensions={0} | all-to-all | bytes 393216 | tf_op jit(solution)/shard_map/all_to_all | solution.py:261
  20.9 0.1 shard_map.60
  21.0 15.6 %collective-permute-start.1 = (f32[16,16,128]{2,1,0:T(8,128)S(1)}, f32[16,16,128]{2,1,0:T(8,128)S(1)}, u32[]{:S(2)}, u32[]{:S(2)}) collective-permute-start(f32[16,16,128]{2,1,0:T(8,128)S(1)} %shard_map.60), channel_id=1, source_target_pairs={{0,1},{1,0},{2,3},{3,2},{4,5},{5,4},{6,7},{7,6},{8,9},{9,8},{10,11... | collective-permute-start | bytes 393224 | tf_op jit(solution)/shard_map/ppermute | solution.py:290
  36.5 1.0 collective-permute-done.1.got
  37.5 2.3 %shard_map.61 = (f32[32,16,128]{2,1,0:T(8,128)S(1)}, bf16[1024,2048]{1,0:T(8,128)(2,1)S(1)}, f32[16,1024]{1,0:T(8,128)S(1)}) custom-call(f32[16,24,128]{2,1,0:T(8,128)S(1)} %all_to_all.30.recv, f32[16,16,128]{2,1,0:T(8,128)S(1)} %collective-permute-done.1.got), custom_call_target="tpu_custom_call" | custom-call | tf_op jit(solution)/shard_map/pallas_call | solution.py:34
  39.9 16.2 %all_to_all.31.recv = f32[32,16,128]{2,1,0:T(8,128)S(1)} all-to-all(f32[32,16,128]{2,1,0:T(8,128)S(1)} %get-tuple-element.16), channel_id=1, replica_groups=mesh['row'=16,'col'=32] {'col'}, dimensions={0} | all-to-all | bytes 524288 | tf_op jit(solution)/shard_map/all_to_all | solution.py:261
  56.0 0.9 shard_map.62
  56.9 16.2 %all_to_all.32.recv = f32[16,8,128]{2,1,0:T(8,128)S(1)} all-to-all(f32[16,8,128]{2,1,0:T(8,128)S(1)} %get-tuple-element.18), channel_id=1, replica_groups=mesh['row'=16,'col'=32] {'row'}, dimensions={0} | all-to-all | bytes 131072 | tf_op jit(solution)/shard_map/all_to_all | solution.py:261
  73.0 1.1 shard_map.63
  74.2 14.3 %all_to_all.33.recv = f32[32,16,128]{2,1,0:T(8,128)S(1)} all-to-all(f32[32,16,128]{2,1,0:T(8,128)S(1)} %shard_map.63), channel_id=1, replica_groups=mesh['row'=16,'col'=32] {'col'}, dimensions={0} | all-to-all | bytes 524288 | tf_op jit(solution)/shard_map/all_to_all | solution.py:261
  88.4 1.1 shard_map.64
  89.5 11.2 %all_to_all.34.recv = f32[32,8,128]{2,1,0:T(8,128)S(1)} all-to-all(f32[32,8,128]{2,1,0:T(8,128)S(1)} %get-tuple-element.26), channel_id=1, replica_groups=mesh['row'=16,'col'=32] {'col'}, dimensions={0} | all-to-all | bytes 262144 | tf_op jit(solution)/shard_map/all_to_all | solution.py:261
  100.7 14.3 %all_to_all.35.recv = f32[16,8,128]{2,1,0:T(8,128)S(1)} all-to-all(f32[16,8,128]{2,1,0:T(8,128)S(1)} %shard_map.65), channel_id=1, replica_groups=mesh['row'=16,'col'=32] {'row'}, dimensions={0} | all-to-all | bytes 131072 | tf_op jit(solution)/shard_map/all_to_all | solution.py:261
  115.0 1.8 %shard_map.66 = (f32[16,64]{1,0:T(8,128)}, f32[16,64]{1,0:T(8,128)}) custom-call(f32[16,8,128]{2,1,0:T(8,128)S(1)} %all_to_all.35.recv, f32[16,32]{1,0:T(8,128)S(1)} %get-tuple-element.27.known, f32[32,64]{1,0:T(8,128)S(1)} %get-tuple-element.28.basis, f32[32,64]{1,0:T(8,128)S(1)} %get-tuple-element.29.images, f32[24,64]{1,0:T(8,128)S(1)} %pad_add_fusion.block), custom_call_target="tpu_custom_call" | custom-call | tf_op jit(solution)/shard_map/pallas_call | solution.py:34
  (1 shorter events, 0.0 us)
Async XLA Ops:
  1.4 9.6 %collective-permute-start = (f32[24,64]{1,0:T(8,128)S(1)}, f32[24,64]{1,0:T(8,128)S(1)}, u32[]{:S(2)}, u32[]{:S(2)}) collective-permute-start(f32[24,64]{1,0:T(8,128)S(1)} %pad_add_fusion.block), channel_id=1, source_target_pairs={{0,1},{1,0},{2,3},{3,2},{4,5},{5,4},{6,7},{7,6},{8,9},{9,8},{10,11... | collective-permute-start | bytes 18440 | tf_op jit(solution)/shard_map/ppermute | solution.py:286
  21.0 16.6 %collective-permute-start.1 = (f32[16,16,128]{2,1,0:T(8,128)S(1)}, f32[16,16,128]{2,1,0:T(8,128)S(1)}, u32[]{:S(2)}, u32[]{:S(2)}) collective-permute-start(f32[16,16,128]{2,1,0:T(8,128)S(1)} %shard_map.60), channel_id=1, source_target_pairs={{0,1},{1,0},{2,3},{3,2},{4,5},{5,4},{6,7},{7,6},{8,9},{9,8},{10,11... | collective-permute-start | bytes 393224 | tf_op jit(solution)/shard_map/ppermute | solution.py:290

commit v6 on v5

--- a/solution.py
+++ b/solution.py
@@ -161,8 +161,8 @@
     high = p.astype(BF16)
     split[0:16] = high
     split[16:32] = (p - high.astype(F32)).astype(BF16)
-    mean = jnp.broadcast_to(jnp.sum(src[4:5, :], 1, keepdims=True), (16, 16))
-    extra = jnp.concatenate([mm_t(p, p), mean, jnp.zeros((16, 32), F32)], 1)
+    mean = jnp.broadcast_to(jnp.sum(src[4:5, :], 1, keepdims=True), (4, 64))
+    extra = jnp.concatenate(quarters(mm_t(p, p)) + [mean], 1)
     for step in range(right.shape[1] // 256):
         lanes = slice(step * 256, step * 256 + 256)
         dist2 = jnp.dot(left[...], right[:, lanes], preferred_element_type=F32)
@@ -170,22 +170,39 @@
     image(split, tile, extra, out)
 
 
+def quarters(x):
+    return [x[i : i + 4] for i in range(0, 16, 4)]
+
+
 def image(split, tile, extra, out):
     both = jnp.dot(split[...], tile[...], preferred_element_type=F32)
     sums = both[:16] + both[16:]
     for i in range(out.shape[0]):
-        out[i, :, :64] = sums[:, i * 64 : i * 64 + 64]
-        out[i, :, 64:] = extra
+        part = quarters(sums[:, i * 64 : i * 64 + 64])
+        for k in range(4):
+            out[i, k // 2, :, 64 * (k % 2) : 64 * (k % 2) + 64] = part[k]
+        out[i, 2] = extra
+
+
+def collect(ref):
+    total = tree_sum(ref)
+    first, second, extra = total[0], total[1], total[2]
+    parts = [first[:, :64], first[:, 64:], second[:, :64], second[:, 64:]]
+    return jnp.concatenate(parts, 0), extra
+
+
+def square_of(extra, lane):
+    return jnp.concatenate([extra[:, lane + 16 * i : lane + 16 * i + 16] for i in range(4)], 0)
 
 
 def second_kernel(
     panels, recv, block, power_near, out, v_near, v_own, w_own, u_own, theta, factor, tmp
 ):
-    total = tree_sum(recv)
-    gram = total[:, 64:80]
-    mean = total[0:1, 80:96] * (1.0 / panels)
+    sums, extra = collect(recv)
+    gram = square_of(extra, 0)
+    mean = extra[0:1, 64:80] * (1.0 / panels)
     p = block[0:16, :]
-    u = (block[20:21, :] - mean[0:1, 0:1]) * p + total[:, :64]
+    u = (block[20:21, :] - mean[0:1, 0:1]) * p + sums
     both = eliminate(gram, jnp.concatenate([identity(16), u], 1), True)
     inverse, u = both[:, :16], both[:, 16:]
     tmp[:, :64] = u[:8]
@@ -205,20 +222,17 @@
     high = u.astype(BF16)
     u_split[0:16] = high
     u_split[16:32] = (u - high.astype(F32)).astype(BF16)
-    extra = jnp.concatenate(
-        [mm_t(v_near[...], u), mm_t(u, u), jnp.zeros((16, 32), F32)], 1
-    )
+    extra = jnp.concatenate(quarters(mm_t(v_near[...], u)) + quarters(mm_t(u, u)), 1)
     image(u_split, tile, extra, out)
 
 
 def fifth_kernel(
     recv, block, v_own, w_own, u_own, theta, factor, out, known, basis, images, tmp
 ):
-    sums = tree_sum(recv)
-    shifted = sums[:, 64:80]
-    gram = sums[:, 80:96]
+    sums, extra = collect(recv)
+    shifted, gram = square_of(extra, 0), square_of(extra, 64)
     v, w, u = v_own[...], w_own[...], u_own[...]
-    x = block[20:21, :] * u + sums[:, :64]
+    x = block[20:21, :] * u + sums
     both = jnp.concatenate([x, u], 1) - t_mm(shifted, jnp.concatenate([w, v], 1))
     both = eliminate(gram - t_mm(shifted, shifted), both, True)
     small = mm_t(jnp.concatenate([w, both[:, :64], block[0:16, :]], 0), both[:, :64])
@@ -290,7 +304,7 @@
     got = lax.ppermute(other, "col", twins)
     parts, tile, power_near = call(
         functools.partial(first_kernel, scale, delta2),
-        [((cols, 16, 128), F32), ((n_near, n_far), BF16), ((nrhs, n_near), F32)],
+        [((cols, 3, 4, 128), F32), ((n_near, n_far), BF16), ((nrhs, n_near), F32)],
         recv, got,
         scratch=[
             pltpu.VMEM((n_near, 32), BF16),
@@ -307,7 +321,7 @@
     )
     recv = exchange(chunk, "row")
     (parts,) = call(
-        third_kernel, [((cols, 16, 128), F32)], recv, v_near, tile,
+        third_kernel, [((cols, 3, 4, 128), F32)], recv, v_near, tile,
         scratch=[pltpu.VMEM((2 * nrhs, n_near), BF16)],
     )
     recv = exchange(parts, "col")

time: 117 us -> 116 us (level)
  blocking collectives: 81.9 us -> 80.4 us
    all_to_all x6, blocking collectives: 81.9 us -> 80.4 us  [exchange(): return lax.all_to_all(parts, axis, 0, 0, axis_index_groups=groups)]
where the time goes in v6:
time: 116 us; the launch traced here: 115 us
  blocking collectives  80.4 us (69%)
  starting transfers between devices  24.4 us (21%)
  Pallas kernels  7.36 us (6%)
  waiting for transfers between devices  1.78 us (2%)
    all_to_all x6, blocking collectives, exchange(): return lax.all_to_all(parts, axis, 0, 0, axis_index_groups=groups)  80.4 us
    ppermute x1, starting transfers between devices, body(): got = lax.ppermute(other, 'col', twins)  15.6 us
    ppermute x1, starting transfers between devices, body(): twin = lax.ppermute(block, 'col', twins)  8.77 us
    pallas_call x8, Pallas kernels, call(): pl.pallas_call(fn, out_shape=tuple((jax.ShapeDtypeStruct(shape, dtype) fo...  7.36 us
  transfers between devices with their start and end apart: 2, of which 2 were waited for; matrix products, arithmetic and copies ran while one was open for 0% of the time, Pallas kernels for 0%

profile of v6, /device:TPU:1, one launch (start us, length us, event | category | flops | bytes accessed | tf_op | source)
XLA Modules:
  0.0 115.4 jit_solution(4074016520961405740)
XLA Ops:
  0.6 0.8 pad_add_fusion.block
  1.4 8.8 %collective-permute-start = (f32[24,64]{1,0:T(8,128)S(1)}, f32[24,64]{1,0:T(8,128)S(1)}, u32[]{:S(2)}, u32[]{:S(2)}) collective-permute-start(f32[24,64]{1,0:T(8,128)S(1)} %pad_add_fusion.block), channel_id=1, source_target_pairs={{0,1},{1,0},{2,3},{3,2},{4,5},{5,4},{6,7},{7,6},{8,9},{9,8},{10,11... | collective-permute-start | bytes 18440 | tf_op jit(solution)/shard_map/ppermute | solution.py:300
  10.2 0.8 collective-permute-done.twin
  11.0 0.1 shard_map.59
  11.1 9.8 %all_to_all.30.recv = f32[16,24,128]{2,1,0:T(8,128)S(1)} all-to-all(f32[16,24,128]{2,1,0:T(8,128)S(1)} %shard_map.59), channel_id=1, replica_groups={{0,32,64,96,128,160,192,224,256,288,320,352,384,416,448,480},{2,34,66,9..., dimensions={0} | all-to-all | bytes 393216 | tf_op jit(solution)/shard_map/all_to_all | solution.py:275
  20.9 0.1 shard_map.60
  21.0 15.6 %collective-permute-start.1 = (f32[16,16,128]{2,1,0:T(8,128)S(1)}, f32[16,16,128]{2,1,0:T(8,128)S(1)}, u32[]{:S(2)}, u32[]{:S(2)}) collective-permute-start(f32[16,16,128]{2,1,0:T(8,128)S(1)} %shard_map.60), channel_id=1, source_target_pairs={{0,1},{1,0},{2,3},{3,2},{4,5},{5,4},{6,7},{7,6},{8,9},{9,8},{10,11... | collective-permute-start | bytes 393224 | tf_op jit(solution)/shard_map/ppermute | solution.py:304
  36.5 1.0 collective-permute-done.1.got
  37.5 2.3 %shard_map.61 = (f32[32,3,4,128]{3,2,1,0:T(4,128)S(1)}, bf16[1024,2048]{1,0:T(8,128)(2,1)S(1)}, f32[16,1024]{1,0:T(8,128)S(1)}) custom-call(f32[16,24,128]{2,1,0:T(8,128)S(1)} %all_to_all.30.recv, f32[16,16,128]{2,1,0:T(8,128)S(1)} %collective-permute-done.1.got), custom_call_target="tpu_custom_call" | custom-call | tf_op jit(solution)/shard_map/pallas_call | solution.py:34
  39.8 15.5 %all_to_all.31.recv = f32[32,3,4,128]{3,2,1,0:T(4,128)S(1)} all-to-all(f32[32,3,4,128]{3,2,1,0:T(4,128)S(1)} %get-tuple-element.16), channel_id=1, replica_groups=mesh['row'=16,'col'=32] {'col'}, dimensions={0} | all-to-all | bytes 393216 | tf_op jit(solution)/shard_map/all_to_all | solution.py:275
  55.3 0.9 shard_map.62
  56.2 16.2 %all_to_all.32.recv = f32[16,8,128]{2,1,0:T(8,128)S(1)} all-to-all(f32[16,8,128]{2,1,0:T(8,128)S(1)} %get-tuple-element.18), channel_id=1, replica_groups=mesh['row'=16,'col'=32] {'row'}, dimensions={0} | all-to-all | bytes 131072 | tf_op jit(solution)/shard_map/all_to_all | solution.py:275
  72.4 1.1 shard_map.63
  73.5 13.5 %all_to_all.33.recv = f32[32,3,4,128]{3,2,1,0:T(4,128)S(1)} all-to-all(f32[32,3,4,128]{3,2,1,0:T(4,128)S(1)} %shard_map.63), channel_id=1, replica_groups=mesh['row'=16,'col'=32] {'col'}, dimensions={0} | all-to-all | bytes 393216 | tf_op jit(solution)/shard_map/all_to_all | solution.py:275
  87.0 1.1 shard_map.64
  88.1 11.2 %all_to_all.34.recv = f32[32,8,128]{2,1,0:T(8,128)S(1)} all-to-all(f32[32,8,128]{2,1,0:T(8,128)S(1)} %get-tuple-element.26), channel_id=1, replica_groups=mesh['row'=16,'col'=32] {'col'}, dimensions={0} | all-to-all | bytes 262144 | tf_op jit(solution)/shard_map/all_to_all | solution.py:275
  99.3 14.3 %all_to_all.35.recv = f32[16,8,128]{2,1,0:T(8,128)S(1)} all-to-all(f32[16,8,128]{2,1,0:T(8,128)S(1)} %shard_map.65), channel_id=1, replica_groups=mesh['row'=16,'col'=32] {'row'}, dimensions={0} | all-to-all | bytes 131072 | tf_op jit(solution)/shard_map/all_to_all | solution.py:275
  113.6 1.8 %shard_map.66 = (f32[16,64]{1,0:T(8,128)}, f32[16,64]{1,0:T(8,128)}) custom-call(f32[16,8,128]{2,1,0:T(8,128)S(1)} %all_to_all.35.recv, f32[16,32]{1,0:T(8,128)S(1)} %get-tuple-element.27.known, f32[32,64]{1,0:T(8,128)S(1)} %get-tuple-element.28.basis, f32[32,64]{1,0:T(8,128)S(1)} %get-tuple-element.29.images, f32[24,64]{1,0:T(8,128)S(1)} %pad_add_fusion.block), custom_call_target="tpu_custom_call" | custom-call | tf_op jit(solution)/shard_map/pallas_call | solution.py:34
  (1 shorter events, 0.0 us)
Async XLA Ops:
  1.4 9.6 %collective-permute-start = (f32[24,64]{1,0:T(8,128)S(1)}, f32[24,64]{1,0:T(8,128)S(1)}, u32[]{:S(2)}, u32[]{:S(2)}) collective-permute-start(f32[24,64]{1,0:T(8,128)S(1)} %pad_add_fusion.block), channel_id=1, source_target_pairs={{0,1},{1,0},{2,3},{3,2},{4,5},{5,4},{6,7},{7,6},{8,9},{9,8},{10,11... | collective-permute-start | bytes 18440 | tf_op jit(solution)/shard_map/ppermute | solution.py:300
  21.0 16.6 %collective-permute-start.1 = (f32[16,16,128]{2,1,0:T(8,128)S(1)}, f32[16,16,128]{2,1,0:T(8,128)S(1)}, u32[]{:S(2)}, u32[]{:S(2)}) collective-permute-start(f32[16,16,128]{2,1,0:T(8,128)S(1)} %shard_map.60), channel_id=1, source_target_pairs={{0,1},{1,0},{2,3},{3,2},{4,5},{5,4},{6,7},{7,6},{8,9},{9,8},{10,11... | collective-permute-start | bytes 393224 | tf_op jit(solution)/shard_map/ppermute | solution.py:304

commit v7 on v6

--- a/solution.py
+++ b/solution.py
@@ -235,10 +235,13 @@
     x = block[20:21, :] * u + sums
     both = jnp.concatenate([x, u], 1) - t_mm(shifted, jnp.concatenate([w, v], 1))
     both = eliminate(gram - t_mm(shifted, shifted), both, True)
-    small = mm_t(jnp.concatenate([w, both[:, :64], block[0:16, :]], 0), both[:, :64])
-    tmp[...] = jnp.zeros_like(tmp)
-    for i in range(6):
-        tmp[:, i * 16 : i * 16 + 16] = small[i * 8 : i * 8 + 8]
+    image2 = both[:, :64]
+    lower = mm_t(image2, jnp.concatenate([w, image2, block[0:16, :]], 0))
+    upper = mm_t(w, image2)
+    tmp[:, 0:48] = lower[:8]
+    tmp[:, 48:96] = lower[8:]
+    tmp[:, 96:112] = upper[:8]
+    tmp[:, 112:128] = upper[8:]
     spread_out(out, tmp[...])
     images[0:16] = w
     images[16:32] = both[:, :64]
@@ -255,14 +258,12 @@
 
 def last_kernel(recv, known, basis, images, block, sol, res):
     total = tree_sum(recv)
-    n12, n22, q2 = (
-        jnp.concatenate([total[:, i : i + 16], total[:, i + 16 : i + 32]], 0)
-        for i in (0, 32, 64)
-    )
+    n12 = jnp.concatenate([total[:, 96:112], total[:, 112:128]], 0)
     system = jnp.concatenate(
         [
             jnp.concatenate([known[:, 0:16], n12, known[:, 16:32]], 1),
-            jnp.concatenate([n12.T, n22, q2.T], 1),
+            total[:, 0:48],
+            total[:, 48:96],
         ],
         0,
     )

time: 116 us -> 116 us (level)
  no operation moved by 1% of the time
where the time goes in v7:
time: 116 us; the launch traced here: 115 us
  blocking collectives  80.4 us (69%)
  starting transfers between devices  24.4 us (21%)
  Pallas kernels  7.31 us (6%)
  waiting for transfers between devices  1.78 us (2%)
    all_to_all x6, blocking collectives, exchange(): return lax.all_to_all(parts, axis, 0, 0, axis_index_groups=groups)  80.4 us
    ppermute x1, starting transfers between devices, body(): got = lax.ppermute(other, 'col', twins)  15.6 us
    ppermute x1, starting transfers between devices, body(): twin = lax.ppermute(block, 'col', twins)  8.77 us
    pallas_call x8, Pallas kernels, call(): pl.pallas_call(fn, out_shape=tuple((jax.ShapeDtypeStruct(shape, dtype) fo...  7.31 us
  transfers between devices with their start and end apart: 2, of which 2 were waited for; matrix products, arithmetic and copies ran while one was open for 0% of the time, Pallas kernels for 0%

profile of v7, /device:TPU:1, one launch (start us, length us, event | category | flops | bytes accessed | tf_op | source)
XLA Modules:
  0.0 115.3 jit_solution(2436033153694129349)
XLA Ops:
  0.6 0.8 pad_add_fusion.block
  1.4 8.8 %collective-permute-start = (f32[24,64]{1,0:T(8,128)S(1)}, f32[24,64]{1,0:T(8,128)S(1)}, u32[]{:S(2)}, u32[]{:S(2)}) collective-permute-start(f32[24,64]{1,0:T(8,128)S(1)} %pad_add_fusion.block), channel_id=1, source_target_pairs={{0,1},{1,0},{2,3},{3,2},{4,5},{5,4},{6,7},{7,6},{8,9},{9,8},{10,11... | collective-permute-start | bytes 18440 | tf_op jit(solution)/shard_map/ppermute | solution.py:301
  10.2 0.8 collective-permute-done.twin
  11.0 0.1 shard_map.59
  11.1 9.8 %all_to_all.30.recv = f32[16,24,128]{2,1,0:T(8,128)S(1)} all-to-all(f32[16,24,128]{2,1,0:T(8,128)S(1)} %shard_map.59), channel_id=1, replica_groups={{0,32,64,96,128,160,192,224,256,288,320,352,384,416,448,480},{2,34,66,9..., dimensions={0} | all-to-all | bytes 393216 | tf_op jit(solution)/shard_map/all_to_all | solution.py:276
  20.9 0.1 shard_map.60
  21.0 15.6 %collective-permute-start.1 = (f32[16,16,128]{2,1,0:T(8,128)S(1)}, f32[16,16,128]{2,1,0:T(8,128)S(1)}, u32[]{:S(2)}, u32[]{:S(2)}) collective-permute-start(f32[16,16,128]{2,1,0:T(8,128)S(1)} %shard_map.60), channel_id=1, source_target_pairs={{0,1},{1,0},{2,3},{3,2},{4,5},{5,4},{6,7},{7,6},{8,9},{9,8},{10,11... | collective-permute-start | bytes 393224 | tf_op jit(solution)/shard_map/ppermute | solution.py:305
  36.5 1.0 collective-permute-done.1.got
  37.5 2.3 %shard_map.61 = (f32[32,3,4,128]{3,2,1,0:T(4,128)S(1)}, bf16[1024,2048]{1,0:T(8,128)(2,1)S(1)}, f32[16,1024]{1,0:T(8,128)S(1)}) custom-call(f32[16,24,128]{2,1,0:T(8,128)S(1)} %all_to_all.30.recv, f32[16,16,128]{2,1,0:T(8,128)S(1)} %collective-permute-done.1.got), custom_call_target="tpu_custom_call" | custom-call | tf_op jit(solution)/shard_map/pallas_call | solution.py:34
  39.8 15.5 %all_to_all.31.recv = f32[32,3,4,128]{3,2,1,0:T(4,128)S(1)} all-to-all(f32[32,3,4,128]{3,2,1,0:T(4,128)S(1)} %get-tuple-element.16), channel_id=1, replica_groups=mesh['row'=16,'col'=32] {'col'}, dimensions={0} | all-to-all | bytes 393216 | tf_op jit(solution)/shard_map/all_to_all | solution.py:276
  55.3 0.9 shard_map.62
  56.2 16.2 %all_to_all.32.recv = f32[16,8,128]{2,1,0:T(8,128)S(1)} all-to-all(f32[16,8,128]{2,1,0:T(8,128)S(1)} %get-tuple-element.18), channel_id=1, replica_groups=mesh['row'=16,'col'=32] {'row'}, dimensions={0} | all-to-all | bytes 131072 | tf_op jit(solution)/shard_map/all_to_all | solution.py:276
  72.4 1.1 shard_map.63
  73.5 13.5 %all_to_all.33.recv = f32[32,3,4,128]{3,2,1,0:T(4,128)S(1)} all-to-all(f32[32,3,4,128]{3,2,1,0:T(4,128)S(1)} %shard_map.63), channel_id=1, replica_groups=mesh['row'=16,'col'=32] {'col'}, dimensions={0} | all-to-all | bytes 393216 | tf_op jit(solution)/shard_map/all_to_all | solution.py:276
  87.0 1.1 shard_map.64
  88.1 11.2 %all_to_all.34.recv = f32[32,8,128]{2,1,0:T(8,128)S(1)} all-to-all(f32[32,8,128]{2,1,0:T(8,128)S(1)} %get-tuple-element.26), channel_id=1, replica_groups=mesh['row'=16,'col'=32] {'col'}, dimensions={0} | all-to-all | bytes 262144 | tf_op jit(solution)/shard_map/all_to_all | solution.py:276
  99.4 14.3 %all_to_all.35.recv = f32[16,8,128]{2,1,0:T(8,128)S(1)} all-to-all(f32[16,8,128]{2,1,0:T(8,128)S(1)} %shard_map.65), channel_id=1, replica_groups=mesh['row'=16,'col'=32] {'row'}, dimensions={0} | all-to-all | bytes 131072 | tf_op jit(solution)/shard_map/all_to_all | solution.py:276
  113.6 1.7 %shard_map.66 = (f32[16,64]{1,0:T(8,128)}, f32[16,64]{1,0:T(8,128)}) custom-call(f32[16,8,128]{2,1,0:T(8,128)S(1)} %all_to_all.35.recv, f32[16,32]{1,0:T(8,128)S(1)} %get-tuple-element.27.known, f32[32,64]{1,0:T(8,128)S(1)} %get-tuple-element.28.basis, f32[32,64]{1,0:T(8,128)S(1)} %get-tuple-element.29.images, f32[24,64]{1,0:T(8,128)S(1)} %pad_add_fusion.block), custom_call_target="tpu_custom_call" | custom-call | tf_op jit(solution)/shard_map/pallas_call | solution.py:34
  (1 shorter events, 0.0 us)
Async XLA Ops:
  1.4 9.6 %collective-permute-start = (f32[24,64]{1,0:T(8,128)S(1)}, f32[24,64]{1,0:T(8,128)S(1)}, u32[]{:S(2)}, u32[]{:S(2)}) collective-permute-start(f32[24,64]{1,0:T(8,128)S(1)} %pad_add_fusion.block), channel_id=1, source_target_pairs={{0,1},{1,0},{2,3},{3,2},{4,5},{5,4},{6,7},{7,6},{8,9},{9,8},{10,11... | collective-permute-start | bytes 18440 | tf_op jit(solution)/shard_map/ppermute | solution.py:301
  21.0 16.6 %collective-permute-start.1 = (f32[16,16,128]{2,1,0:T(8,128)S(1)}, f32[16,16,128]{2,1,0:T(8,128)S(1)}, u32[]{:S(2)}, u32[]{:S(2)}) collective-permute-start(f32[16,16,128]{2,1,0:T(8,128)S(1)} %shard_map.60), channel_id=1, source_target_pairs={{0,1},{1,0},{2,3},{3,2},{4,5},{5,4},{6,7},{7,6},{8,9},{9,8},{10,11... | collective-permute-start | bytes 393224 | tf_op jit(solution)/shard_map/ppermute | solution.py:305
